TPU v7x, 32 devices: a whole 2x2x4 slice. The times are simulated.
32 devices in a mesh: dp: 8 (over z, x), tensor: 4 (over y, core).
Axes of the slice: x: 2, y: 2, z: 4, core: 2. Of those that a mesh axis runs over, the one named last changes fastest.
Arguments:
- frames: bfloat16 [4096, 768], P(('dp', 'tensor')), may hold values from -6 to 6
- clip_offsets: int32 [6], replicated, may hold values from 0 to 4095, as said below
- qkv_weight: bfloat16 [1, 768, 3, 768], P(None, 'dp', None, 'tensor'), may hold values from -0.3125 to 0.3125
- out_weight: bfloat16 [1, 768, 768], P(None, 'tensor', 'dp'), may hold values from -1.25 to 1.25
- up_weight: bfloat16 [1, 768, 3072], P(None, 'dp', 'tensor'), may hold values from -0.21875 to 0.21875
- down_weight: bfloat16 [1, 3072, 768], P(None, 'tensor', 'dp'), may hold values from -0.15625 to 0.15625
- ln_gain: float32 [1, 2, 768], replicated, may hold values from 0.1 to 1.9
- ln_bias: float32 [1, 2, 768], replicated, may hold values from -1.8 to 1.8
- proj_bias: float32 [1, 4, 768], replicated, may hold values from -1.8 to 1.8
- fc_bias: float32 [1, 3072], replicated, may hold values from -3 to 3
- out_cotangent: bfloat16 [4096, 768], P(('dp', 'tensor')), may hold values from -6 to 6
Outputs:
- encoded: bfloat16 [4096, 768], P(('dp', 'tensor'))
- frames_grad: bfloat16 [4096, 768], P(('dp', 'tensor'))
- qkv_grad: float32 [1, 768, 3, 768], P(None, 'dp', None, 'tensor')
- out_grad: float32 [1, 768, 768], P(None, 'tensor', 'dp')
- up_grad: float32 [1, 768, 3072], P(None, 'dp', 'tensor')
- down_grad: float32 [1, 3072, 768], P(None, 'tensor', 'dp')
- ln_gain_grad: float32 [1, 2, 768], replicated
- ln_bias_grad: float32 [1, 2, 768], replicated
- proj_bias_grad: float32 [1, 4, 768], replicated
- fc_bias_grad: float32 [1, 3072], replicated
Inputs may be any that keep to these rules, and one draw needn't show every extreme that they name: clip_offsets[0] is 0 and the offsets rise; a clip runs from its offset up to the next one (the last up to 4096), holds at most 1500 frames, and some clip holds exactly 1500.
All inputs are finite; a program needn't handle non-finite values.
Results may differ from a plain program's by a relative error of at most 0.014.
The roundings to bfloat16 on the way count: a program that leaves them out, or rounds other values in their place, can miss the bound.
Values may be sent and summed in bfloat16 or wider, within the bound.
A program may use at most 128 MiB of HBM per device.

v0:
```python
from functools import partial

import jax
import jax.numpy as jnp
from jax import lax
from jax.sharding import PartitionSpec as P

D = 768
HEAD = 64
FF = 3072
REACH = 3


EPSILON = 1e-05


def passed_along(value, axis, steps):
    count = lax.axis_size(axis)
    initial, last = (max(0, -steps), min(count, count - steps))
    return lax.ppermute(value, axis, [(source, source + steps) for source in range(initial, last)])


def norm_rows(values, gains, shifts):
    average = jnp.mean(values, axis=-1, keepdims=True)
    centered = values - average
    variance = jnp.mean(centered * centered, axis=-1, keepdims=True)
    return centered * lax.rsqrt(variance + EPSILON) * gains + shifts


def clip_ids(positions, clip_offsets):
    return jnp.sum((positions[:, None] >= clip_offsets[None, :]).astype(jnp.int32), axis=1) - 1


def contract_rows(left, right):
    return lax.dot_general(
        left, right, (((0,), (0,)), ((), ())), preferred_element_type=jnp.float32
    )


def contract_cols(left, right):
    return lax.dot_general(
        left, right, (((1,), (1,)), ((), ())), preferred_element_type=jnp.float32
    )


def gather_rows(values):
    return lax.all_gather(values, "tensor", axis=0, tiled=True)


def gather_grads(values):
    return lax.all_gather(values, "tensor", axis=0, tiled=True)


def reduce_rows(left, right, local_rows):

    def term(start, count):
        return jnp.dot(left, right, preferred_element_type=jnp.float32)

    return lax.psum_scatter(
        term(jnp.int32(0), local_rows * lax.axis_size("tensor")),
        "tensor",
        scatter_dimension=0,
        tiled=True,
    )


def reduce_grads(left, right, local_rows):

    def term(start, count):
        return contract_cols(left, right)

    return lax.psum_scatter(
        term(jnp.int32(0), local_rows * lax.axis_size("tensor")),
        "tensor",
        scatter_dimension=0,
        tiled=True,
    )


def attention_mask(dp_idx, dp_count, group_rows, clip_offsets):
    window = (2 * REACH + 1) * group_rows
    query_pos = dp_idx * group_rows + jnp.arange(group_rows, dtype=jnp.int32)
    key_pos = (dp_idx - REACH) * group_rows + jnp.arange(window, dtype=jnp.int32)
    inside = (key_pos >= 0) & (key_pos < dp_count * group_rows)
    same_clip = (
        clip_ids(query_pos, clip_offsets)[:, None] == clip_ids(key_pos, clip_offsets)[None, :]
    )
    return same_clip & inside[None, :]


def head_scores(queries, all_keys, allowed):
    group_rows = queries.shape[0]
    heads_here = queries.shape[1] // HEAD
    scores = jnp.einsum(
        "qhd,khd->hqk",
        queries.reshape(group_rows, heads_here, HEAD),
        all_keys.reshape(all_keys.shape[0], heads_here, HEAD),
        preferred_element_type=jnp.float32,
    ) * HEAD ** (-0.5)
    return jnp.where(allowed[None], scores, -1000000000.0)


def attention_forward(normed_group, qkv_full, pbias, tensor_idx, allowed):
    group_rows = normed_group.shape[0]
    local_width = qkv_full.shape[2]
    heads_here = local_width // HEAD
    projected = jnp.einsum(
        "nd,dkh->nkh", normed_group, qkv_full, preferred_element_type=jnp.float32
    )
    query_bias = lax.dynamic_slice_in_dim(pbias[0], tensor_idx * local_width, local_width)
    value_bias = lax.dynamic_slice_in_dim(pbias[1], tensor_idx * local_width, local_width)
    bias_rows = jnp.stack([query_bias, jnp.zeros_like(query_bias), value_bias])
    projected = (projected + bias_rows[None]).astype(jnp.bfloat16)
    queries = projected[:, 0]
    own_keys = projected[:, 1]
    own_values = projected[:, 2]
    key_parts = []
    value_parts = []
    for offset_gap in range(-REACH, REACH + 1):
        if offset_gap == 0:
            key_parts.append(own_keys)
            value_parts.append(own_values)
        else:
            near_keys, near_values = passed_along((own_keys, own_values), "dp", -offset_gap)
            key_parts.append(near_keys)
            value_parts.append(near_values)
    all_keys = jnp.concatenate(key_parts, axis=0)
    values = jnp.concatenate(value_parts, axis=0)
    masked = head_scores(queries, all_keys, allowed)
    largest = jnp.max(masked, axis=-1, keepdims=True)
    weights = jnp.exp(masked - largest)
    totals = jnp.sum(weights, axis=-1, keepdims=True)
    attn_probs = (weights / totals).astype(jnp.bfloat16)
    log_total = largest + jnp.log(totals)
    attended = jnp.einsum(
        "hqk,khd->qhd",
        attn_probs,
        values.reshape(-1, heads_here, HEAD),
        preferred_element_type=jnp.float32,
    )
    attended = attended.reshape(group_rows, local_width).astype(jnp.bfloat16)
    return (queries, all_keys, values, log_total, attended)


def attention_backward(grad_attended, queries, all_keys, values, allowed, log_total):
    group_rows = queries.shape[0]
    local_width = queries.shape[1]
    heads_here = local_width // HEAD
    head_scale = HEAD ** (-0.5)
    masked = head_scores(queries, all_keys, allowed)
    attn_probs = jnp.exp(masked - log_total)
    grad_heads = grad_attended.reshape(group_rows, heads_here, HEAD)
    grad_probs = jnp.einsum(
        "qhd,khd->hqk",
        grad_heads,
        values.reshape(-1, heads_here, HEAD),
        preferred_element_type=jnp.float32,
    )
    inner_sum = jnp.sum(attn_probs * grad_probs, axis=-1, keepdims=True)
    grad_scores = (attn_probs * (grad_probs - inner_sum)).astype(jnp.bfloat16)
    grad_queries = (
        jnp.einsum(
            "hqk,khd->qhd",
            grad_scores,
            all_keys.reshape(-1, heads_here, HEAD),
            preferred_element_type=jnp.float32,
        )
        * head_scale
    )
    grad_keys = (
        jnp.einsum(
            "hqk,qhd->khd",
            grad_scores,
            queries.reshape(group_rows, heads_here, HEAD),
            preferred_element_type=jnp.float32,
        )
        * head_scale
    )
    grad_values = jnp.einsum(
        "hqk,qhd->khd",
        attn_probs.astype(jnp.bfloat16),
        grad_heads,
        preferred_element_type=jnp.float32,
    )
    grad_keys = grad_keys.reshape(2 * REACH + 1, group_rows, local_width)
    grad_values = grad_values.reshape(2 * REACH + 1, group_rows, local_width)
    total_keys = grad_keys[REACH]
    total_values = grad_values[REACH]
    for offset_gap in range(-REACH, REACH + 1):
        if offset_gap != 0:
            back_keys, back_values = passed_along(
                (grad_keys[offset_gap + REACH], grad_values[offset_gap + REACH]), "dp", offset_gap
            )
            total_keys = total_keys + back_keys
            total_values = total_values + back_values
    return (grad_queries.reshape(group_rows, local_width), total_keys, total_values)


def layer_forward(state, fetched, gains, shifts, pbias, fbias, tensor_idx, allowed):
    qkv_full, out_full, up_full, down_full = fetched
    local_rows = state.shape[0]
    normed = norm_rows(state, gains[0], shifts[0]).astype(jnp.bfloat16)
    normed_group = gather_rows(normed)
    queries, all_keys, values, log_total, attended = attention_forward(
        normed_group, qkv_full, pbias, tensor_idx, allowed
    )
    hidden = state + (reduce_rows(attended, out_full, local_rows) + pbias[2])
    normed_two = norm_rows(hidden, gains[1], shifts[1]).astype(jnp.bfloat16)
    normed_two_group = gather_rows(normed_two)
    hidden_width = up_full.shape[1]
    upper = jnp.dot(normed_two_group, up_full, preferred_element_type=jnp.float32)
    upper = upper + lax.dynamic_slice_in_dim(fbias, tensor_idx * hidden_width, hidden_width)
    activated = jax.nn.gelu(upper, approximate=False).astype(jnp.bfloat16)
    output = hidden + (reduce_rows(activated, down_full, local_rows) + pbias[3])
    kept = (
        state,
        hidden,
        normed_group,
        queries,
        all_keys,
        values,
        log_total,
        attended,
        normed_two_group,
        upper,
        activated,
    )
    return (output, kept)


def place_slice(piece, tensor_idx, full_width):
    return lax.dynamic_update_slice_in_dim(
        jnp.zeros((full_width,), jnp.float32), piece, tensor_idx * piece.shape[0], 0
    )


def layer_backward(grad_state, fetched, kept, gains, shifts, tensor_idx, allowed):
    qkv_full, out_full, up_full, down_full = fetched
    (
        state,
        hidden,
        normed_group,
        queries,
        all_keys,
        values,
        log_total,
        attended,
        normed_two_group,
        upper,
        activated,
    ) = kept
    local_rows = state.shape[0]
    grad_mlp = grad_state.astype(jnp.bfloat16)
    down_bias_grad = jnp.sum(grad_mlp, axis=0, dtype=jnp.float32)
    grad_mlp_group = gather_grads(grad_mlp)
    down_grad = contract_rows(activated, grad_mlp_group)
    grad_act = contract_cols(grad_mlp_group, down_full)
    gelu_back = jax.vjp(partial(jax.nn.gelu, approximate=False), upper)[1]
    grad_upper = gelu_back(grad_act)[0].astype(jnp.bfloat16)
    fc_grad = place_slice(jnp.sum(grad_upper, axis=0, dtype=jnp.float32), tensor_idx, FF)
    up_grad = contract_rows(normed_two_group, grad_upper)
    grad_normed_two = reduce_grads(grad_upper, up_full, local_rows)
    norm_back_two = jax.vjp(norm_rows, hidden, gains[1], shifts[1])[1]
    grad_hidden_add, gain_two_grad, shift_two_grad = norm_back_two(grad_normed_two)
    grad_hidden = grad_state + grad_hidden_add
    grad_branch = grad_hidden.astype(jnp.bfloat16)
    out_bias_grad = jnp.sum(grad_branch, axis=0, dtype=jnp.float32)
    grad_branch_group = gather_grads(grad_branch)
    out_grad = contract_rows(attended, grad_branch_group)
    grad_attended = contract_cols(grad_branch_group, out_full).astype(jnp.bfloat16)
    grad_queries, total_keys, total_values = attention_backward(
        grad_attended, queries, all_keys, values, allowed, log_total
    )
    grad_proj = jnp.stack([grad_queries, total_keys, total_values], axis=1).astype(jnp.bfloat16)
    group_rows = grad_proj.shape[0]
    local_width = grad_proj.shape[2]
    qkv_grad = jnp.einsum(
        "nd,nkh->dkh", normed_group, grad_proj, preferred_element_type=jnp.float32
    )
    bias_sums = jnp.sum(grad_proj, axis=0, dtype=jnp.float32)
    query_bias_grad = place_slice(bias_sums[0], tensor_idx, D)
    value_bias_grad = place_slice(bias_sums[2], tensor_idx, D)
    grad_normed = reduce_grads(
        grad_proj.reshape(group_rows, 3 * local_width),
        qkv_full.reshape(qkv_full.shape[0], 3 * local_width),
        local_rows,
    )
    norm_back_one = jax.vjp(norm_rows, state, gains[0], shifts[0])[1]
    grad_state_add, gain_one_grad, shift_one_grad = norm_back_one(grad_normed)
    new_grad = grad_hidden + grad_state_add
    qkv_grad, out_grad, up_grad, down_grad = (
        lax.psum_scatter(qkv_grad, "dp", scatter_dimension=0, tiled=True),
        lax.psum_scatter(out_grad, "dp", scatter_dimension=1, tiled=True),
        lax.psum_scatter(up_grad, "dp", scatter_dimension=0, tiled=True),
        lax.psum_scatter(down_grad, "dp", scatter_dimension=1, tiled=True),
    )
    weight_grads = (qkv_grad, out_grad, up_grad, down_grad)
    vector_grads = (
        jnp.stack([gain_one_grad, gain_two_grad]),
        jnp.stack([shift_one_grad, shift_two_grad]),
        jnp.stack([query_bias_grad, value_bias_grad, out_bias_grad, down_bias_grad]),
        fc_grad,
    )
    return (new_grad, weight_grads, vector_grads)


def shards(
    frames,
    clip_offsets,
    qkv_weight,
    out_weight,
    up_weight,
    down_weight,
    ln_gain,
    ln_bias,
    proj_bias,
    fc_bias,
    out_cotangent,
):
    tensor_idx = lax.axis_index("tensor")
    dp_idx = lax.axis_index("dp")
    dp_count = lax.axis_size("dp")
    tensor_count = lax.axis_size("tensor")
    group_rows = frames.shape[0] * tensor_count
    allowed = attention_mask(dp_idx, dp_count, group_rows, clip_offsets)
    state = frames.astype(jnp.float32)
    layer_idx = 0
    fetched = (
        lax.all_gather(qkv_weight[layer_idx], "dp", axis=0, tiled=True),
        lax.all_gather(out_weight[layer_idx], "dp", axis=1, tiled=True),
        lax.all_gather(up_weight[layer_idx], "dp", axis=0, tiled=True),
        lax.all_gather(down_weight[layer_idx], "dp", axis=1, tiled=True),
    )
    state, kept = layer_forward(
        state,
        fetched,
        ln_gain[layer_idx],
        ln_bias[layer_idx],
        proj_bias[layer_idx],
        fc_bias[layer_idx],
        tensor_idx,
        allowed,
    )
    saved_layers = [kept]
    encoded = state.astype(jnp.bfloat16)
    grad_state = out_cotangent.astype(jnp.float32)
    weight_list = []
    vector_list = []
    layer_idx = 0
    fetched = (
        lax.all_gather(qkv_weight[layer_idx], "dp", axis=0, tiled=True),
        lax.all_gather(out_weight[layer_idx], "dp", axis=1, tiled=True),
        lax.all_gather(up_weight[layer_idx], "dp", axis=0, tiled=True),
        lax.all_gather(down_weight[layer_idx], "dp", axis=1, tiled=True),
    )
    grad_state, weight_grads, vector_grads = layer_backward(
        grad_state,
        fetched,
        saved_layers[layer_idx],
        ln_gain[layer_idx],
        ln_bias[layer_idx],
        tensor_idx,
        allowed,
    )
    weight_list.append(weight_grads)
    vector_list.append(vector_grads)
    weight_list = weight_list[::-1]
    vector_list = vector_list[::-1]
    stacked = tuple((jnp.stack([entry[member] for entry in weight_list]) for member in range(4)))
    vector_stacks = tuple(
        (jnp.stack([entry[member] for entry in vector_list]) for member in range(4))
    )
    gain_grads, shift_grads, pbias_grads, fbias_grads = lax.psum(
        (vector_stacks[0], vector_stacks[1], vector_stacks[2], vector_stacks[3]), ("dp", "tensor")
    )
    frames_grad = grad_state.astype(jnp.bfloat16)
    return (
        encoded,
        frames_grad,
        stacked[0],
        stacked[1],
        stacked[2],
        stacked[3],
        gain_grads,
        shift_grads,
        pbias_grads,
        fbias_grads,
    )


def solution(mesh):
    return jax.shard_map(
        shards,
        mesh=mesh,
        in_specs=(
            P(("dp", "tensor"), None),
            P(),
            P(None, "dp", None, "tensor"),
            P(None, "tensor", "dp"),
            P(None, "dp", "tensor"),
            P(None, "tensor", "dp"),
            P(),
            P(),
            P(),
            P(),
            P(("dp", "tensor"), None),
        ),
        out_specs=(
            P(("dp", "tensor"), None),
            P(("dp", "tensor"), None),
            P(None, "dp", None, "tensor"),
            P(None, "tensor", "dp"),
            P(None, "dp", "tensor"),
            P(None, "tensor", "dp"),
            P(),
            P(),
            P(),
            P(),
        ),
        check_vma=False,
    )
```

profile of v0, /device:TPU:0, one launch (start us, length us, event | category | flops | bytes accessed | tf_op | source)
XLA Modules:
  0.0 759.9 jit_solution(8104846611664933329)
XLA Ops:
  15.5 10.5 %all_gather.28 = bf16[512,768]{1,0:T(8,128)(2,1)} all-gather(bf16[128,768]{1,0:T(8,128)(2,1)S(1)} %fusion.37), channel_id=1, replica_groups=mesh['dp'=8,'tensor'=4] {'tensor'}, dimensions={0}, use_global_device_ids=true | all-gather | bytes 983040 | tf_op jit(solution)/shard_map/all_gather | solution.py:47
  26.0 38.0 %all-gather = bf16[1,768,3,192]{3,2,0,1:T(4,128)(2,1)S(1)} all-gather(bf16[1,96,3,192]{3,2,0,1:T(4,128)(2,1)S(1)} %copy.32), channel_id=2, replica_groups=mesh['dp'=8,'tensor'=4] {'dp'}, dimensions={1}, use_global_device_ids=true | all-gather | bytes 995328 | tf_op jit(solution)/shard_map/all_gather | solution.py:329
  87.3 33.0 %all-gather.1 = bf16[1,192,768]{1,0,2:T(2,128)(2,1)S(1)} all-gather(bf16[1,192,96]{1,0,2:T(2,128)(2,1)S(1)} %copy.34), channel_id=3, replica_groups=mesh['dp'=8,'tensor'=4] {'dp'}, dimensions={2}, use_global_device_ids=true | all-gather | bytes 331776 | tf_op jit(solution)/shard_map/all_gather | solution.py:330
  130.0 7.8 %collective-permute-done.9 = bf16[512,192]{0,1:T(8,128)(2,1)S(1)} collective-permute-done((bf16[512,192]{0,1:T(8,128)(2,1)S(1)}, bf16[512,192]{0,1:T(8,128)(2,1)S(1)}, u32[]{:S(2)}, u32[]{:S(2)}) %collective-permute-start.9) | collective-permute-done | bytes 196640 | tf_op jit(solution)/shard_map/ppermute | solution.py:20
  161.9 7.3 copy-done.2
  173.0 9.8 %fusion.26 = bf16[3,64,512]{2,1,0:T(8,128)(2,1)S(1)} fusion(bf16[3584,3,64]{0,2,1:T(8,128)(2,1)} %copy-done.11, f32[3,512,3584]{2,1,0:T(8,128)} %copy-done.2, f32[3,512]{1,0:T(4,128)S(1)} %fusion, f32[3,512]{1,0:T(4,128)S(1)} %get-tuple-element.61), kind=kOutput, calls=%fused_computation.48 | convolution fusion | flops 721256448 | bytes 23605248 | tf_op jit(solution)/shard_map/hqk,khd->qhd/dot_general | solution.py:135
  185.8 8.2 %all_gather.34 = bf16[512,768]{1,0:T(8,128)(2,1)S(1)} all-gather(bf16[128,768]{1,0:T(8,128)(2,1)S(1)} %copy-done.13), channel_id=1, replica_groups=mesh['dp'=8,'tensor'=4] {'tensor'}, dimensions={0}, use_global_device_ids=true | all-gather | bytes 983040 | tf_op jit(solution)/shard_map/all_gather | solution.py:51
  194.0 21.4 %reduce-scatter.11.cloned.1.call-done = f32[128,768]{1,0:T(8,128)} async-done(((f32[512,768]{1,0:T(8,128)}), f32[128,768]{1,0:T(8,128)}) %reduce-scatter.11.cloned.1.call-update) | async-done | bytes 393232 | tf_op jit(solution)/shard_map/reduce_scatter | solution.py:59
  217.0 8.4 %all_gather.31 = bf16[512,768]{1,0:T(8,128)(2,1)S(1)} all-gather(bf16[128,768]{1,0:T(8,128)(2,1)S(1)} %add_convert_fusion.4), channel_id=1, replica_groups=mesh['dp'=8,'tensor'=4] {'tensor'}, dimensions={0}, use_global_device_ids=true | all-gather | bytes 983040 | tf_op jit(solution)/shard_map/all_gather | solution.py:47
  237.8 35.7 %all-gather.9.cloned.1.call-done = bf16[1,768,768]{1,2,0:T(8,128)(2,1)} async-done(((bf16[1,768,96]{1,2,0:T(8,128)(2,1)}), bf16[1,768,768]{1,2,0:T(8,128)(2,1)}) %all-gather.9.cloned.1.call-update) | async-done | bytes 1179664 | tf_op jit(solution)/shard_map/all_gather | solution.py:332
  284.2 23.2 %reduce-scatter.15.cloned.1.call-done = f32[128,768]{1,0:T(8,128)} async-done(((f32[512,768]{1,0:T(8,128)}), f32[128,768]{1,0:T(8,128)}) %reduce-scatter.15.cloned.1.call-update) | async-done | bytes 393232 | tf_op jit(solution)/shard_map/reduce_scatter | solution.py:72
  309.2 28.9 %reduce-scatter.13.cloned.1.call-done = f32[128,768]{1,0:T(8,128)} async-done(((f32[512,768]{1,0:T(8,128)}), f32[128,768]{1,0:T(8,128)}) %reduce-scatter.13.cloned.1.call-update) | async-done | bytes 393232 | tf_op jit(solution)/shard_map/reduce_scatter | solution.py:59
  340.9 8.2 %all_gather.35 = bf16[512,768]{1,0:T(8,128)(2,1)S(1)} all-gather(bf16[128,768]{1,0:T(8,128)(2,1)S(1)} %get-tuple-element.28), channel_id=1, replica_groups=mesh['dp'=8,'tensor'=4] {'tensor'}, dimensions={0}, use_global_device_ids=true | all-gather | bytes 983040 | tf_op jit(solution)/shard_map/all_gather | solution.py:51
  349.5 9.3 %fusion.6 = f32[3584,3,64]{0,2,1:T(8,128)S(1)} fusion(bf16[512,3,64]{0,2,1:T(8,128)(2,1)S(1)} %bitcast.150, f32[3,512,3584]{2,1,0:T(8,128)} %copy-done.2, f32[3,512]{1,0:T(4,128)S(1)} %log_add_fusion), kind=kOutput, calls=%fused_computation.13 | convolution fusion | flops 715653120 | bytes 24975360 | tf_op jit(solution)/shard_map/hqk,qhd->khd/dot_general | solution.py:179
  358.8 13.8 %multiply_reduce_fusion = (f32[3,512]{1,0:T(4,128)S(1)}, f32[3,512,3584]{2,1,0:T(8,128)}) fusion(f32[3,512,3584]{2,1,0:T(8,128)} %copy-done.2, f32[3,512]{1,0:T(4,128)S(1)} %log_add_fusion, bf16[512,3,64]{0,2,1:T(8,128)(2,1)S(1)} %bitcast.151, bf16[3584,3,64]{0,2,1:T(8,128)(2,1)S(1)} %copy-done.12), kind=kOutput, calls=%fused_computation.1 | convolution fusion | flops 721156608 | bytes 45625344 | tf_op jit(solution)/shard_map/qhd,khd->hqk/dot_general | solution.py:153
  389.3 15.1 %multiply_convert_fusion = bf16[3,512,3584]{2,1,0:T(8,128)(2,1)S(1)} fusion(f32[3,512,3584]{2,1,0:T(8,128)} %get-tuple-element.65, f32[3,512,3584]{2,1,0:T(8,128)} %copy-done.2, f32[3,512]{1,0:T(4,128)S(1)} %get-tuple-element.64, f32[3,512]{1,0:T(4,128)S(1)} %log_add_fusion), kind=kLoop, calls=%fused_computation | loop fusion | flops 22020096 | bytes 55062528 | tf_op jit(solution)/shard_map/convert_element_type | solution.py:160
  411.3 8.0 %collective-permute-start.17 = (f32[512,192]{0,1:T(8,128)}, f32[512,192]{0,1:T(8,128)}, u32[]{:S(2)}, u32[]{:S(2)}) collective-permute-start(f32[512,192]{0,1:T(8,128)} %bitcast.37), channel_id=1, source_target_pairs={{0,12},{4,16},{8,20},{12,24},{16,28},{1,13},{5,17},{9,21},{13,25},... | collective-permute-start | bytes 1179656 | tf_op jit(solution)/shard_map/ppermute | solution.py:20
  437.1 8.0 %fusion.25 = bf16[3,64,512]{2,1,0:T(8,128)(2,1)S(1)} fusion(bf16[3584,3,64]{0,2,1:T(8,128)(2,1)} %copy-done.8, bf16[3,512,3584]{2,1,0:T(8,128)(2,1)} %copy-done.3), kind=kOutput, calls=%fused_computation.46 | convolution fusion | flops 704839680 | bytes 12582912 | tf_op jit(solution)/shard_map/hqk,khd->qhd/dot_general | solution.py:162
  473.4 30.2 %reduce-scatter.25.cloned.1.call-done = f32[96,192]{1,0:T(8,128)} async-done(((f32[768,192]{1,0:T(8,128)}), f32[96,192]{1,0:T(8,128)}) %reduce-scatter.25.cloned.1.call-update) | async-done | bytes 73744
  505.3 28.1 %reduce-scatter.17.cloned.1.call-done = f32[128,768]{1,0:T(8,128)} async-done(((f32[512,768]{1,0:T(8,128)}), f32[128,768]{1,0:T(8,128)}) %reduce-scatter.17.cloned.1.call-update) | async-done | bytes 393232 | tf_op jit(solution)/shard_map/reduce_scatter | solution.py:72
  537.9 41.4 %all-reduce = (f32[1,2,768]{2,1,0:T(2,128)}, f32[1,2,768]{2,1,0:T(2,128)}, f32[1,4,768]{2,1,0:T(4,128)}, f32[1,3072]{1,0:T(1,128)}) all-reduce(f32[1,2,768]{2,1,0:T(2,128)S(1)} %maximum_bitcast_fusion.1, f32[1,2,768]{2,1,0:T(2,128)S(1)} %maximum_bitcast_fusion.2, ...), channel_id=1, replica_groups=mesh['dp'=8,'tensor'=4] {'dp','tensor'}, use_global_device_ids=true, to_apply=%region_23.24 | all-reduce | flops 9216 | bytes 73728 | tf_op jit(solution)/shard_map/psum | solution.py:373
  579.3 28.6 %reduce-scatter.23.cloned.1.call-done = f32[768,96]{0,1:T(8,128)} async-done(((f32[768,768]{0,1:T(8,128)}), f32[768,96]{0,1:T(8,128)}) %reduce-scatter.23.cloned.1.call-update) | async-done | bytes 294928 | tf_op jit(solution)/shard_map/reduce_scatter | solution.py:295
  607.9 72.5 %reduce-scatter.21.cloned.1.call-done = f32[96,768]{1,0:T(8,128)} async-done(((f32[768,768]{1,0:T(8,128)}), f32[96,768]{1,0:T(8,128)}) %reduce-scatter.21.cloned.1.call-update) | async-done | bytes 294928 | tf_op jit(solution)/shard_map/reduce_scatter | solution.py:294
  680.4 72.4 %reduce-scatter.19.cloned.1.call-done = f32[96,3,192]{2,0,1:T(8,128)} async-done(((f32[768,3,192]{2,0,1:T(8,128)}), f32[96,3,192]{2,0,1:T(8,128)}) %reduce-scatter.19.cloned.1.call-update) | async-done | bytes 221200 | tf_op jit(solution)/shard_map/reduce_scatter | solution.py:292
  (231 shorter events, 175.8 us)
Async XLA Ops:
  8.0 207.4 %reduce-scatter.11.cloned.1.call-start = ((), (), s32[]{:S(2)}) async-start(), calls=%async_computation.8 | async-start | bytes 1966080 | tf_op jit(solution)/shard_map/reduce_scatter | solution.py:59
  67.4 87.1 %collective-permute-start.5 = (bf16[512,192]{0,1:T(8,128)(2,1)S(1)}, bf16[512,192]{0,1:T(8,128)(2,1)S(1)}, u32[]{:S(2)}, u32[]{:S(2)}) collective-permute-start(bf16[512,192]{0,1:T(8,128)(2,1)S(1)} %get-tuple-element.50), channel_id=1, source_target_pairs={{12,0},{16,4},{20,8},{24,12},{28,16},{13,1},{17,5},{21,9},{25,13},... | collective-permute-start | bytes 589832 | tf_op jit(solution)/shard_map/ppermute | solution.py:20
  68.7 85.7 %collective-permute-start.4 = (bf16[512,192]{0,1:T(8,128)(2,1)S(1)}, bf16[512,192]{0,1:T(8,128)(2,1)S(1)}, u32[]{:S(2)}, u32[]{:S(2)}) collective-permute-start(bf16[512,192]{0,1:T(8,128)(2,1)S(1)} %get-tuple-element.50), channel_id=1, source_target_pairs={{8,0},{12,4},{16,8},{20,12},{24,16},{28,20},{9,1},{13,5},{17,9},{2... | collective-permute-start | bytes 589832 | tf_op jit(solution)/shard_map/ppermute | solution.py:20
  70.0 84.4 %collective-permute-start.3 = (bf16[512,192]{0,1:T(8,128)(2,1)S(1)}, bf16[512,192]{0,1:T(8,128)(2,1)S(1)}, u32[]{:S(2)}, u32[]{:S(2)}) collective-permute-start(bf16[512,192]{0,1:T(8,128)(2,1)S(1)} %get-tuple-element.50), channel_id=1, source_target_pairs={{4,0},{8,4},{12,8},{16,12},{20,16},{24,20},{28,24},{5,1},{9,5},{13... | collective-permute-start | bytes 589832 | tf_op jit(solution)/shard_map/ppermute | solution.py:20
  71.3 51.9 %collective-permute-start = (bf16[512,192]{0,1:T(8,128)(2,1)S(1)}, bf16[512,192]{0,1:T(8,128)(2,1)S(1)}, u32[]{:S(2)}, u32[]{:S(2)}) collective-permute-start(bf16[512,192]{0,1:T(8,128)(2,1)S(1)} %get-tuple-element.50), channel_id=1, source_target_pairs={{0,12},{4,16},{8,20},{12,24},{16,28},{1,13},{5,17},{9,21},{13,25},... | collective-permute-start | bytes 589832 | tf_op jit(solution)/shard_map/ppermute | solution.py:20
  78.1 43.9 %collective-permute-start.6 = (bf16[512,192]{0,1:T(8,128)(2,1)S(1)}, bf16[512,192]{0,1:T(8,128)(2,1)S(1)}, u32[]{:S(2)}, u32[]{:S(2)}) collective-permute-start(bf16[512,192]{0,1:T(8,128)(2,1)S(1)} %get-tuple-element.51), channel_id=1, source_target_pairs={{0,12},{4,16},{8,20},{12,24},{16,28},{1,13},{5,17},{9,21},{13,25},... | collective-permute-start | bytes 589832 | tf_op jit(solution)/shard_map/ppermute | solution.py:20
  184.5 46.7 %all-gather.7.cloned.1.call-start = ((), (), s32[]{:S(2)}) async-start(), calls=%async_computation.15 | async-start | bytes 1327104 | tf_op jit(solution)/shard_map/all_gather | solution.py:331
  185.1 88.4 %all-gather.9.cloned.1.call-start = ((), (), s32[]{:S(2)}) async-start(), calls=%async_computation.16 | async-start | bytes 1327104 | tf_op jit(solution)/shard_map/all_gather | solution.py:332
  185.7 121.7 %reduce-scatter.15.cloned.1.call-start = ((), (), s32[]{:S(2)}) async-start(), calls=%async_computation.10 | async-start | bytes 1966080 | tf_op jit(solution)/shard_map/reduce_scatter | solution.py:72
  280.6 57.6 %reduce-scatter.13.cloned.1.call-start = ((), (), s32[]{:S(2)}) async-start(), calls=%async_computation.9 | async-start | bytes 1966080 | tf_op jit(solution)/shard_map/reduce_scatter | solution.py:59
  284.1 219.5 %reduce-scatter.25.cloned.1.call-start = ((), (), s32[]{:S(2)}) async-start(), calls=%async_computation.17 | async-start | bytes 884736
  373.9 36.1 %collective-permute-start.23 = (f32[512,192]{0,1:T(8,128)S(1)}, f32[512,192]{0,1:T(8,128)}, u32[]{:S(2)}, u32[]{:S(2)}) collective-permute-start(f32[512,192]{0,1:T(8,128)S(1)} %bitcast.171), channel_id=1, source_target_pairs={{0,12},{4,16},{8,20},{12,24},{16,28},{1,13},{5,17},{9,21},{13,25},... | collective-permute-start | bytes 1179656 | tf_op jit(solution)/shard_map/ppermute | solution.py:20
  378.9 32.4 %collective-permute-start.22 = (f32[512,192]{0,1:T(8,128)S(1)}, f32[512,192]{0,1:T(8,128)}, u32[]{:S(2)}, u32[]{:S(2)}) collective-permute-start(f32[512,192]{0,1:T(8,128)S(1)} %bitcast.170), channel_id=1, source_target_pairs={{0,8},{4,12},{8,16},{12,20},{16,24},{20,28},{1,9},{5,13},{9,17},{1... | collective-permute-start | bytes 1179656 | tf_op jit(solution)/shard_map/ppermute | solution.py:20
  383.1 37.7 %collective-permute-start.21 = (f32[512,192]{0,1:T(8,128)}, f32[512,192]{0,1:T(8,128)}, u32[]{:S(2)}, u32[]{:S(2)}) collective-permute-start(f32[512,192]{0,1:T(8,128)} %bitcast.44), channel_id=1, source_target_pairs={{0,4},{4,8},{8,12},{12,16},{16,20},{20,24},{24,28},{1,5},{5,9},{9,... | collective-permute-start | bytes 1179656 | tf_op jit(solution)/shard_map/ppermute | solution.py:20
  386.4 37.9 %collective-permute-start.20 = (f32[512,192]{0,1:T(8,128)}, f32[512,192]{0,1:T(8,128)}, u32[]{:S(2)}, u32[]{:S(2)}) collective-permute-start(f32[512,192]{0,1:T(8,128)} %bitcast.43), channel_id=1, source_target_pairs={{4,0},{8,4},{12,8},{16,12},{20,16},{24,20},{28,24},{5,1},{9,5},{13... | collective-permute-start | bytes 1179656 | tf_op jit(solution)/shard_map/ppermute | solution.py:20
  387.7 41.3 %collective-permute-start.19 = (f32[512,192]{0,1:T(8,128)}, f32[512,192]{0,1:T(8,128)}, u32[]{:S(2)}, u32[]{:S(2)}) collective-permute-start(f32[512,192]{0,1:T(8,128)} %bitcast.42), channel_id=1, source_target_pairs={{8,0},{12,4},{16,8},{20,12},{24,16},{28,20},{9,1},{13,5},{17,9},{2... | collective-permute-start | bytes 1179656 | tf_op jit(solution)/shard_map/ppermute | solution.py:20
  411.3 24.5 %collective-permute-start.17 = (f32[512,192]{0,1:T(8,128)}, f32[512,192]{0,1:T(8,128)}, u32[]{:S(2)}, u32[]{:S(2)}) collective-permute-start(f32[512,192]{0,1:T(8,128)} %bitcast.37), channel_id=1, source_target_pairs={{0,12},{4,16},{8,20},{12,24},{16,28},{1,13},{5,17},{9,21},{13,25},... | collective-permute-start | bytes 1179656 | tf_op jit(solution)/shard_map/ppermute | solution.py:20
  420.7 112.7 %reduce-scatter.17.cloned.1.call-start = ((), (), s32[]{:S(2)}) async-start(), calls=%async_computation.11 | async-start | bytes 1966080 | tf_op jit(solution)/shard_map/reduce_scatter | solution.py:72
  420.8 26.3 %collective-permute-start.16 = (f32[512,192]{0,1:T(8,128)}, f32[512,192]{0,1:T(8,128)S(1)}, u32[]{:S(2)}, u32[]{:S(2)}) collective-permute-start(f32[512,192]{0,1:T(8,128)} %bitcast.169), channel_id=1, source_target_pairs={{0,8},{4,12},{8,16},{12,20},{16,24},{20,28},{1,9},{5,13},{9,17},{1... | collective-permute-start | bytes 1179656 | tf_op jit(solution)/shard_map/ppermute | solution.py:20
  424.3 25.2 %collective-permute-start.15 = (f32[512,192]{0,1:T(8,128)}, f32[512,192]{0,1:T(8,128)S(1)}, u32[]{:S(2)}, u32[]{:S(2)}) collective-permute-start(f32[512,192]{0,1:T(8,128)} %bitcast.168), channel_id=1, source_target_pairs={{0,4},{4,8},{8,12},{12,16},{16,20},{20,24},{24,28},{1,5},{5,9},{9,... | collective-permute-start | bytes 1179656 | tf_op jit(solution)/shard_map/ppermute | solution.py:20
  430.3 23.3 %collective-permute-start.13 = (f32[512,192]{0,1:T(8,128)}, f32[512,192]{0,1:T(8,128)S(1)}, u32[]{:S(2)}, u32[]{:S(2)}) collective-permute-start(f32[512,192]{0,1:T(8,128)} %bitcast.166), channel_id=1, source_target_pairs={{8,0},{12,4},{16,8},{20,12},{24,16},{28,20},{9,1},{13,5},{17,9},{2... | collective-permute-start | bytes 1179656 | tf_op jit(solution)/shard_map/ppermute | solution.py:20
  461.7 146.1 %reduce-scatter.23.cloned.1.call-start = ((), (), s32[]{:S(2)}) async-start(), calls=%async_computation.14 | async-start | bytes 2654208 | tf_op jit(solution)/shard_map/reduce_scatter | solution.py:295
  465.1 215.3 %reduce-scatter.21.cloned.1.call-start = ((), (), s32[]{:S(2)}) async-start(), calls=%async_computation.13 | async-start | bytes 2654208 | tf_op jit(solution)/shard_map/reduce_scatter | solution.py:294
  468.5 284.4 %reduce-scatter.19.cloned.1.call-start = ((), (), s32[]{:S(2)}) async-start(), calls=%async_computation.12 | async-start | bytes 2654208 | tf_op jit(solution)/shard_map/reduce_scatter | solution.py:292
  (46 other events, 1225.2 us)
Sparse Core Ops, SparseCore 0:
  184.7 30.7 reduce-scatter.10
  280.7 26.6 reduce-scatter.14
  309.9 28.1 reduce-scatter.12
Sparse Core Ops, SparseCore 1:
  187.4 43.7 all-gather.6
  233.5 40.0 all-gather.8
  420.8 82.8 reduce-scatter.24
  506.2 27.1 reduce-scatter.16
  537.9 69.9 reduce-scatter.22
  612.4 68.0 reduce-scatter.20
  684.7 68.0 reduce-scatter.18
where the time goes:
time: 762 us; the launch traced here: 760 us
  waiting for transfers between devices  383 us (50%)
  blocking collectives  148 us (19%)
  matrix products  79.4 us (10%)
  starting transfers between devices  66.8 us (9%)
  other arithmetic  39 us (5%)
  local copies, waits for them, and re-layouts  27.6 us (4%)
  between operations  16.3 us (2%)
    reduce_scatter x1, waiting for transfers between devices, layer_backward(): lax.psum_scatter(up_grad, 'dp', scatter_dimension=0, tiled=True)  72.5 us
    reduce_scatter x1, waiting for transfers between devices, layer_backward(): lax.psum_scatter(qkv_grad, 'dp', scatter_dimension=0, tiled=True)  72.4 us
    ppermute x24, starting transfers between devices, passed_along(): lax.ppermute(value, axis, [(source, source + steps) for source in range(i...  66.4 us
    reduce_scatter x2, waiting for transfers between devices, reduce_grads(): lax.psum_scatter(term(jnp.int32(0), local_rows * lax.axis_size('tensor'))...  51.3 us
    reduce_scatter x2, waiting for transfers between devices, reduce_rows(): lax.psum_scatter(term(jnp.int32(0), local_rows * lax.axis_size('tensor'))...  50.4 us
    psum x1, blocking collectives, shards(): lax.psum((vector_stacks[0], vector_stacks[1], vector_stacks[2], vector_st...  41.4 us
    all_gather x1, blocking collectives, shards(): lax.all_gather(qkv_weight[layer_idx], 'dp', axis=0, tiled=True)  38 us
    all_gather x1, waiting for transfers between devices, shards(): lax.all_gather(down_weight[layer_idx], 'dp', axis=1, tiled=True)  35.7 us
  transfers between devices with their start and end apart: 34, of which 19 were waited for; matrix products, arithmetic and copies ran while one was open for 9% of the time, Pallas kernels for 0%

commit v1 on v0

v1 whole, which is shorter than its diff:
```python
from functools import partial

import jax
import jax.numpy as jnp
from jax import lax
from jax.experimental import pallas as pl
from jax.experimental.pallas import tpu as pltpu
from jax.sharding import PartitionSpec as P

D = 768
HEAD = 64
REACH = 3
EPSILON = 1e-05
MESH = pl.DeviceIdType.MESH
F32 = jnp.float32
BF16 = jnp.bfloat16
VMEM = pl.BlockSpec(memory_space=pltpu.VMEM)
LIMIT = 56 * 1024 * 1024


def dma(n):
    return pltpu.SemaphoreType.DMA((n,))


def send(src, dst, send_sem, recv_sem, where):
    return pltpu.make_async_remote_copy(
        src_ref=src, dst_ref=dst, send_sem=send_sem, recv_sem=recv_sem,
        device_id=where, device_id_type=MESH,
    )


class Place:
    def __init__(self, sizes):
        self.n, self.t_count = sizes
        self.half = self.n // 2
        self.dp = lax.axis_index("dp")
        self.t = lax.axis_index("tensor")
        self.hi = lax.div(self.dp, 2)
        self.lo = lax.rem(self.dp, 2)

    def tensor_at(self, k):
        return lax.rem(self.t + k, self.t_count)

    def tensor_back(self, k):
        return lax.rem(self.t + self.t_count - k, self.t_count)

    def hi_at(self, k):
        return lax.rem(self.hi + k, self.half)

    def hi_back(self, k):
        return lax.rem(self.hi + self.half - k, self.half)

    def partner(self):
        return {"dp": self.hi * 2 + 1 - self.lo}

    def along(self, k):
        return {"dp": self.hi_at(k) * 2 + self.lo}


def greet(peers):
    barrier = pltpu.get_barrier_semaphore()
    for peer in peers:
        pl.semaphore_signal(barrier, inc=1, device_id=peer, device_id_type=MESH)
    pl.semaphore_wait(barrier, len(peers))


def tensor_peers(place):
    return [{"tensor": place.tensor_at(k)} for k in range(1, place.t_count)]


def two_level_peers(place):
    return [place.partner()] + [place.along(k) for k in range(1, place.half)]


def tensor_gather_start(place, src, group, ss, rs):
    copies = []
    for k in range(1, place.t_count):
        c = send(src, group.at[place.t], ss.at[k], rs.at[k], {"tensor": place.tensor_at(k)})
        c.start()
        copies.append(c)
    return copies


def tensor_scatter_start(place, part, slots, ss, rs):
    copies = []
    for k in range(1, place.t_count):
        c = send(part.at[place.tensor_at(k)], slots.at[k - 1], ss.at[k], rs.at[k],
                 {"tensor": place.tensor_at(k)})
        c.start()
        copies.append(c)
    return copies


def tensor_scatter_sum(place, part, slots, copies):
    total = part[place.t].astype(F32)
    for k in range(1, place.t_count):
        copies[k - 1].wait()
        total = total + slots[k - 1].astype(F32)
    return total


def gather_start(place, local, full, ss, rs, xs, xr):
    direct = [None]
    forwards = []
    mine = place.dp
    c = send(local, full.at[mine], xs.at[0], xr.at[0], place.partner())
    c.start()
    forwards.append(c)
    for k in range(1, place.half):
        c = send(local, full.at[mine], ss.at[k], rs.at[k], place.along(k))
        c.start()
        direct.append(c)
    return direct, forwards


def gather_finish(place, full, direct, forwards, xs, xr):
    for k in range(1, place.half):
        direct[k].wait_recv()
        got = full.at[place.hi_back(k) * 2 + place.lo]
        c = send(got, got, xs.at[k], xr.at[k], place.partner())
        c.start()
        forwards.append(c)
    for k in range(1, place.half):
        direct[k].wait_send()
    for c in forwards:
        c.wait()


def scatter_start(place, part, rx, xs, xr):
    copies = [None] * place.half
    for k in list(range(1, place.half)) + [0]:
        c = send(part.at[place.hi_at(k) * 2 + 1 - place.lo], rx.at[k], xs.at[k], xr.at[k],
                 place.partner())
        c.start()
        copies[k] = c
    return copies


def scatter_middle(place, part, rx, stage, rz, copies, ss, rs):
    onward = [None]
    for k in range(1, place.half):
        copies[k].wait()
        total = part[place.hi_at(k) * 2 + place.lo].astype(F32) + rx[k].astype(F32)
        stage[k] = total.astype(BF16)
        c = send(stage.at[k], rz.at[k], ss.at[k], rs.at[k], place.along(k))
        c.start()
        onward.append(c)
    copies[0].wait()
    return onward


def scatter_finish(place, part, rx, rz, onward, out):
    total = part[place.hi * 2 + place.lo].astype(F32) + rx[0].astype(F32)
    for k in range(1, place.half):
        onward[k].wait()
        total = total + rz[k].astype(F32)
    out[...] = total


def norm_parts(values):
    average = jnp.mean(values, axis=-1, keepdims=True)
    centered = values - average
    variance = jnp.mean(centered * centered, axis=-1, keepdims=True)
    r = lax.rsqrt(variance + EPSILON)
    return centered * r, r


def norm_back(xhat, r, grad, gain):
    e = grad * gain
    return r * (
        e - jnp.mean(e, axis=-1, keepdims=True)
        - xhat * jnp.mean(e * xhat, axis=-1, keepdims=True)
    )


def column_sum(values):
    return jnp.sum(values, axis=0, keepdims=True)


def open_kernel(sizes, frames, cot, weights, gain, shift, normed_g, cot_g, w_full,
                mine, ns, nr, cs, cr, ws, wr, xs, xr):
    place = Place(sizes)
    greet(tensor_peers(place) + two_level_peers(place))
    direct, forwards = gather_start(place, weights, w_full, ws, wr, xs, xr)
    cots = tensor_gather_start(place, cot, cot_g, cs, cr)
    xhat, _ = norm_parts(frames[...].astype(F32))
    mine[...] = (xhat * gain[...] + shift[...]).astype(BF16)
    normeds = tensor_gather_start(place, mine, normed_g, ns, nr)
    normed_g[place.t] = mine[...]
    cot_g[place.t] = cot[...]
    w_full[place.dp] = weights[...]
    gather_finish(place, w_full, direct, forwards, xs, xr)
    for c in cots + normeds:
        c.wait()


def near_kernel(sizes, kv, window, ss, rs):
    place = Place(sizes)
    n = place.n
    gaps = [g for g in (1, -1, 2, -2, 3, -3)]
    barrier = pltpu.get_barrier_semaphore()
    here = [(place.dp + g >= 0) & (place.dp + g < n) for g in gaps]
    for g, ok in zip(gaps, here):
        @pl.when(ok)
        def _(g=g):
            pl.semaphore_signal(barrier, inc=1, device_id={"dp": place.dp + g},
                                device_id_type=MESH)
    pl.semaphore_wait(barrier, sum(ok.astype(jnp.int32) for ok in here))

    def copy(i, g):
        return send(kv, window.at[REACH - g], ss.at[i], rs.at[i], {"dp": place.dp + g})

    for i, g in enumerate(gaps):
        @pl.when(here[i])
        def _(i=i, g=g):
            copy(i, g).start()
    window[REACH] = kv[...]
    for i, g in enumerate(gaps):
        @pl.when(jnp.logical_not((place.dp - g >= 0) & (place.dp - g < n)))
        def _(g=g):
            window[REACH - g] = jnp.zeros_like(kv)
    for i, g in enumerate(gaps):
        @pl.when(here[i])
        def _(i=i, g=g):
            copy(i, g).wait_send()

        @pl.when((place.dp - g >= 0) & (place.dp - g < n))
        def _(i=i, g=g):
            copy(i, g).wait_recv()


def middle_kernel(sizes, part, frames, gain, shift, bias, hidden, c_g,
                  slots, mine, ps, pr, cs, cr):
    place = Place(sizes)
    greet(tensor_peers(place))
    copies = tensor_scatter_start(place, part, slots, ps, pr)
    h = frames[...].astype(F32) + (tensor_scatter_sum(place, part, slots, copies) + bias[...])
    hidden[...] = h
    xhat, _ = norm_parts(h)
    mine[...] = (xhat * gain[...] + shift[...]).astype(BF16)
    sends = tensor_gather_start(place, mine, c_g, cs, cr)
    c_g[place.t] = mine[...]
    for c in sends:
        c.wait()


def turn_kernel(sizes, down, dc_part, hidden, cot, gain, bias, encoded, dh_out, dz_g, vec,
                slots_d, slots_c, mine, ds, dr, cs, cr, zs, zr):
    place = Place(sizes)
    greet(tensor_peers(place))
    c_copies = tensor_scatter_start(place, dc_part, slots_c, cs, cr)
    d_copies = tensor_scatter_start(place, down, slots_d, ds, dr)
    h = hidden[...]
    xhat, r = norm_parts(h)
    dc = tensor_scatter_sum(place, dc_part, slots_c, c_copies)
    dh = cot[...].astype(F32) + norm_back(xhat, r, dc, gain[...])
    dh_out[...] = dh
    dz = dh.astype(BF16)
    mine[...] = dz
    sends = tensor_gather_start(place, mine, dz_g, zs, zr)
    dz_g[place.t] = dz
    vec[0:1] = column_sum(dc * xhat)
    vec[1:2] = column_sum(dc)
    vec[2:3] = column_sum(dz.astype(F32))
    vec[3:4] = column_sum(cot[...].astype(F32))
    encoded[...] = (
        h + (tensor_scatter_sum(place, down, slots_d, d_copies) + bias[...])
    ).astype(BF16)
    for c in sends:
        c.wait()


def back_kernel(sizes, dkv, grads, dkv_out, grads_out,
                slots, rx, stage, rz, ks, kr, xs, xr, ss, rs):
    place = Place(sizes)
    n = place.n
    gaps = [g for g in (1, -1, 2, -2, 3, -3)]

    def inside(g):
        return (place.dp + g >= 0) & (place.dp + g < n)

    peers = two_level_peers(place)
    barrier = pltpu.get_barrier_semaphore()
    for peer in peers:
        pl.semaphore_signal(barrier, inc=1, device_id=peer, device_id_type=MESH)
    for g in gaps:
        @pl.when(inside(g))
        def _(g=g):
            pl.semaphore_signal(barrier, inc=1, device_id={"dp": place.dp + g},
                                device_id_type=MESH)
    pl.semaphore_wait(barrier, len(peers) + sum(inside(g).astype(jnp.int32) for g in gaps))

    def copy(i, g):
        return send(dkv.at[REACH + g], slots.at[i], ks.at[i], kr.at[i], {"dp": place.dp + g})

    for i, g in enumerate(gaps):
        @pl.when(inside(g))
        def _(i=i, g=g):
            copy(i, g).start()
    copies = scatter_start(place, grads, rx, xs, xr)
    dkv_out[...] = dkv[REACH].astype(F32)
    onward = scatter_middle(place, grads, rx, stage, rz, copies, ss, rs)
    for i, g in enumerate(gaps):
        @pl.when(inside(g))
        def _(i=i, g=g):
            copy(i, g).wait_send()

        @pl.when(inside(-g))
        def _(i=i, g=g):
            copy(i, g).wait_recv()
            dkv_out[...] += slots[i].astype(F32)
    scatter_finish(place, grads, rx, rz, onward, grads_out)


def close_kernel(sizes, da_part, frames, dh, gain, grads, vec_in, frames_grad, grads_out, vec_out,
                 slots, rx, stage, rz, vec, vt, vsum, vx, vpair, vz,
                 ps, pr, xs, xr, ss, rs, vs, vr, us, ur, zs, zr):
    place = Place(sizes)
    greet(tensor_peers(place) + two_level_peers(place))
    copies = tensor_scatter_start(place, da_part, slots, ps, pr)
    x_copies = scatter_start(place, grads, rx, xs, xr)
    xhat, r = norm_parts(frames[...].astype(F32))
    da = tensor_scatter_sum(place, da_part, slots, copies)
    frames_grad[...] = (dh[...] + norm_back(xhat, r, da, gain[...])).astype(BF16)
    vec[...] = vec_in[...]
    vec[0:1] = column_sum(da * xhat)
    vec[2:3] = column_sum(da)
    v_copies = []
    for k in range(1, place.t_count):
        c = send(vec, vt.at[k - 1], vs.at[k], vr.at[k], {"tensor": place.tensor_at(k)})
        c.start()
        v_copies.append(c)
    onward = scatter_middle(place, grads, rx, stage, rz, x_copies, ss, rs)
    for c in v_copies:
        c.wait()
    vsum[place.t] = vec[...]
    for k in range(1, place.t_count):
        vsum[place.tensor_back(k)] = vt[k - 1]
    total = vsum[0]
    for k in range(1, place.t_count):
        total = total + vsum[k]
    vx[0] = total
    c = send(vx.at[0], vx.at[1], us.at[0], ur.at[0], place.partner())
    c.start()
    c.wait()
    vpair[...] = vx[0] + vx[1]
    vz[place.hi] = vpair[...]
    z_copies = []
    for k in range(1, place.half):
        c = send(vpair, vz.at[place.hi], zs.at[k], zr.at[k], place.along(k))
        c.start()
        z_copies.append(c)
    scatter_finish(place, grads, rx, rz, onward, grads_out)
    for c in z_copies:
        c.wait()
    total = vz[0]
    for k in range(1, place.half):
        total = total + vz[k]
    vec_out[...] = total


def call(kernel, sizes, ident, outs, scratch, *args):
    return pl.pallas_call(
        partial(kernel, sizes),
        out_shape=[jax.ShapeDtypeStruct(s, t) for s, t in outs],
        in_specs=[VMEM] * len(args),
        out_specs=[VMEM] * len(outs),
        scratch_shapes=scratch,
        compiler_params=pltpu.CompilerParams(
            collective_id=ident, has_side_effects=True, vmem_limit_bytes=LIMIT
        ),
    )(*args)


def clip_ids(positions, clip_offsets):
    return jnp.sum((positions[:, None] >= clip_offsets[None, :]).astype(jnp.int32), axis=1) - 1


def contract_rows(left, right):
    return lax.dot_general(
        left, right, (((0,), (0,)), ((), ())), preferred_element_type=jnp.float32
    )


def contract_cols(left, right):
    return lax.dot_general(
        left, right, (((1,), (1,)), ((), ())), preferred_element_type=jnp.float32
    )


def attention_mask(dp_idx, dp_count, group_rows, clip_offsets):
    window = (2 * REACH + 1) * group_rows
    query_pos = dp_idx * group_rows + jnp.arange(group_rows, dtype=jnp.int32)
    key_pos = (dp_idx - REACH) * group_rows + jnp.arange(window, dtype=jnp.int32)
    inside = (key_pos >= 0) & (key_pos < dp_count * group_rows)
    same_clip = (
        clip_ids(query_pos, clip_offsets)[:, None] == clip_ids(key_pos, clip_offsets)[None, :]
    )
    return same_clip & inside[None, :]


def head_scores(queries, all_keys, allowed):
    group_rows = queries.shape[0]
    heads_here = queries.shape[1] // HEAD
    scores = jnp.einsum(
        "qhd,khd->hqk",
        queries.reshape(group_rows, heads_here, HEAD),
        all_keys.reshape(all_keys.shape[0], heads_here, HEAD),
        preferred_element_type=jnp.float32,
    ) * HEAD ** (-0.5)
    return jnp.where(allowed[None], scores, -1000000000.0)


def attention_forward(queries, all_keys, values, allowed):
    group_rows, local_width = queries.shape
    heads_here = local_width // HEAD
    masked = head_scores(queries, all_keys, allowed)
    largest = jnp.max(masked, axis=-1, keepdims=True)
    weights = jnp.exp(masked - largest)
    totals = jnp.sum(weights, axis=-1, keepdims=True)
    attn_probs = (weights / totals).astype(BF16)
    log_total = largest + jnp.log(totals)
    attended = jnp.einsum(
        "hqk,khd->qhd", attn_probs, values.reshape(-1, heads_here, HEAD),
        preferred_element_type=F32,
    )
    return log_total, attended.reshape(group_rows, local_width).astype(BF16)


def attention_backward(grad_attended, queries, all_keys, values, allowed, log_total):
    group_rows = queries.shape[0]
    local_width = queries.shape[1]
    heads_here = local_width // HEAD
    head_scale = HEAD ** (-0.5)
    masked = head_scores(queries, all_keys, allowed)
    attn_probs = jnp.exp(masked - log_total)
    grad_heads = grad_attended.reshape(group_rows, heads_here, HEAD)
    grad_probs = jnp.einsum(
        "qhd,khd->hqk", grad_heads, values.reshape(-1, heads_here, HEAD),
        preferred_element_type=F32,
    )
    inner_sum = jnp.sum(attn_probs * grad_probs, axis=-1, keepdims=True)
    grad_scores = (attn_probs * (grad_probs - inner_sum)).astype(BF16)
    grad_queries = jnp.einsum(
        "hqk,khd->qhd", grad_scores, all_keys.reshape(-1, heads_here, HEAD),
        preferred_element_type=F32,
    ) * head_scale
    grad_keys = jnp.einsum(
        "hqk,qhd->khd", grad_scores, queries.reshape(group_rows, heads_here, HEAD),
        preferred_element_type=F32,
    ) * head_scale
    grad_values = jnp.einsum(
        "hqk,qhd->khd", attn_probs.astype(BF16), grad_heads, preferred_element_type=F32,
    )
    shape = (2 * REACH + 1, group_rows, local_width)
    dkv = jnp.concatenate(
        [grad_keys.astype(BF16).reshape(shape), grad_values.astype(BF16).reshape(shape)], axis=2
    )
    return grad_queries.reshape(group_rows, local_width).astype(BF16), dkv


def place_slice(piece, tensor_idx, full_width):
    return lax.dynamic_update_slice_in_dim(
        jnp.zeros((full_width,), F32), piece, tensor_idx * piece.shape[0], 0
    )


def shards(
    frames, clip_offsets, qkv_weight, out_weight, up_weight, down_weight,
    ln_gain, ln_bias, proj_bias, fc_bias, out_cotangent,
):
    t_idx = lax.axis_index("tensor")
    dp_idx = lax.axis_index("dp")
    n = lax.axis_size("dp")
    t_count = lax.axis_size("tensor")
    sizes = (n, t_count)
    half = n // 2
    rows = frames.shape[0]
    group = rows * t_count
    wrows = qkv_weight.shape[1]
    width = qkv_weight.shape[3]
    ff = up_weight.shape[2]
    ff_all = fc_bias.shape[1]
    gains, shifts, pbias, fbias = ln_gain[0], ln_bias[0], proj_bias[0], fc_bias[0]

    w_local = jnp.concatenate(
        [qkv_weight[0].reshape(wrows, 3 * width), out_weight[0].T, up_weight[0], down_weight[0].T],
        axis=1,
    )
    total = w_local.shape[1]
    t3 = (t_count, rows, D)
    normed_g, cot_g, w_full = call(
        open_kernel, sizes, 1,
        [(t3, BF16), (t3, BF16), ((n, wrows, total), BF16)],
        [pltpu.VMEM((rows, D), BF16), dma(t_count), dma(t_count), dma(t_count), dma(t_count),
         dma(half), dma(half), dma(half), dma(half)],
        frames, out_cotangent, w_local, gains[0:1], shifts[0:1],
    )
    normed_g = normed_g.reshape(group, D)
    cot_g = cot_g.reshape(group, D)
    w_full = w_full.reshape(D, total)
    cut = [3 * width, 4 * width, 4 * width + ff]
    qkv_full = w_full[:, :cut[0]]
    out_t = w_full[:, cut[0]:cut[1]]
    up_full = w_full[:, cut[1]:cut[2]]
    down_t = w_full[:, cut[2]:]

    allowed = attention_mask(dp_idx, n, group, clip_offsets)
    q_bias = lax.dynamic_slice_in_dim(pbias[0], t_idx * width, width)
    v_bias = lax.dynamic_slice_in_dim(pbias[1], t_idx * width, width)
    bias_row = jnp.concatenate([q_bias, jnp.zeros_like(q_bias), v_bias])
    projected = (jnp.dot(normed_g, qkv_full, preferred_element_type=F32) + bias_row).astype(BF16)
    queries = projected[:, :width]
    (window,) = call(
        near_kernel, sizes, 2, [((2 * REACH + 1, group, 2 * width), BF16)],
        [dma(6), dma(6)], projected[:, width:],
    )
    window = window.reshape(-1, 2 * width)
    all_keys, values = window[:, :width], window[:, width:]
    log_total, attended = attention_forward(queries, all_keys, values, allowed)

    part = contract_cols(attended, out_t).astype(BF16).reshape(t3)
    hidden, c_g = call(
        middle_kernel, sizes, 3, [((rows, D), F32), (t3, BF16)],
        [pltpu.VMEM((t_count - 1, rows, D), BF16), pltpu.VMEM((rows, D), BF16)]
        + [dma(t_count)] * 4,
        part, frames, gains[1:2], shifts[1:2], pbias[2:3],
    )
    c_g = c_g.reshape(group, D)
    upper = jnp.dot(c_g, up_full, preferred_element_type=F32)
    upper = upper + lax.dynamic_slice_in_dim(fbias, t_idx * ff, ff)
    cdf = 0.5 * (1.0 + lax.erf(upper * (2.0 ** -0.5)))
    activated = (upper * cdf).astype(BF16)
    down_part = contract_cols(activated, down_t).astype(BF16).reshape(t3)

    slope = cdf + upper * jnp.exp(-0.5 * upper * upper) * 0.3989422804014327
    grad_act = jnp.dot(cot_g, down_t, preferred_element_type=F32)
    grad_upper = (grad_act * slope).astype(BF16)
    dc_part = contract_cols(grad_upper, up_full).astype(BF16).reshape(t3)
    encoded, dh, dz_g, vec2 = call(
        turn_kernel, sizes, 4,
        [((rows, D), BF16), ((rows, D), F32), (t3, BF16), ((4, D), F32)],
        [pltpu.VMEM((t_count - 1, rows, D), BF16), pltpu.VMEM((t_count - 1, rows, D), BF16),
         pltpu.VMEM((rows, D), BF16)] + [dma(t_count)] * 6,
        down_part, dc_part, hidden, out_cotangent, gains[1:2], pbias[3:4],
    )
    dz_g = dz_g.reshape(group, D)
    fc_grad = place_slice(jnp.sum(grad_upper, axis=0, dtype=F32), t_idx, ff_all)
    down_grad_t = contract_rows(cot_g, activated)
    up_grad = contract_rows(c_g, grad_upper)
    out_grad_t = contract_rows(dz_g, attended)
    grad_attended = jnp.dot(dz_g, out_t, preferred_element_type=F32).astype(BF16)
    grad_queries, dkv = attention_backward(
        grad_attended, queries, all_keys, values, allowed, log_total
    )
    three = jnp.concatenate([out_grad_t, up_grad, down_grad_t], axis=1).astype(BF16)
    w3 = three.shape[1]
    dkv_sum, three = call(
        back_kernel, sizes, 5, [((group, 2 * width), F32), ((wrows, w3), F32)],
        [pltpu.VMEM((6, group, 2 * width), BF16)] + [pltpu.VMEM((half, wrows, w3), BF16)] * 3
        + [dma(6)] * 2 + [dma(half)] * 4,
        dkv, three.reshape(n, wrows, w3),
    )
    out_grad = three[:, :width].T
    up_grad = three[:, width:width + ff]
    down_grad = three[:, width + ff:].T

    grad_proj = jnp.concatenate([grad_queries, dkv_sum.astype(BF16)], axis=1)
    qkv_grad = contract_rows(normed_g, grad_proj).astype(BF16)
    bias_sums = jnp.sum(grad_proj, axis=0, dtype=F32)
    da_part = contract_cols(grad_proj, qkv_full).astype(BF16).reshape(t3)
    zero = jnp.zeros((1, D), F32)
    vec = jnp.concatenate([
        zero, vec2[0:1], zero, vec2[1:2],
        place_slice(bias_sums[:width], t_idx, D)[None],
        place_slice(bias_sums[2 * width:], t_idx, D)[None],
        vec2[2:4], fc_grad.reshape(-1, D), zero, zero, zero, zero,
    ], axis=0)
    vshape = vec.shape
    frames_grad, qkv_grad, vec = call(
        close_kernel, sizes, 6,
        [((rows, D), BF16), ((wrows, 3 * width), F32), (vshape, F32)],
        [pltpu.VMEM((t_count - 1, rows, D), BF16)]
        + [pltpu.VMEM((half, wrows, 3 * width), BF16)] * 3
        + [pltpu.VMEM(vshape, F32), pltpu.VMEM((t_count - 1,) + vshape, F32),
           pltpu.VMEM((t_count,) + vshape, F32), pltpu.VMEM((2,) + vshape, F32),
           pltpu.VMEM(vshape, F32), pltpu.VMEM((half,) + vshape, F32)]
        + [dma(t_count)] * 2 + [dma(half)] * 4 + [dma(t_count)] * 2 + [dma(1)] * 2
        + [dma(half)] * 2,
        da_part, frames, dh, gains[0:1], qkv_grad.reshape(n, wrows, 3 * width), vec,
    )
    fc_rows = ff_all // D
    return (
        encoded,
        frames_grad,
        qkv_grad.reshape(1, wrows, 3, width),
        out_grad[None],
        up_grad[None],
        down_grad[None],
        vec[None, 0:2],
        vec[None, 2:4],
        vec[None, 4:8],
        vec[8:8 + fc_rows].reshape(1, ff_all),
    )


def solution(mesh):
    return jax.shard_map(
        shards,
        mesh=mesh,
        in_specs=(
            P(("dp", "tensor"), None),
            P(),
            P(None, "dp", None, "tensor"),
            P(None, "tensor", "dp"),
            P(None, "dp", "tensor"),
            P(None, "tensor", "dp"),
            P(),
            P(),
            P(),
            P(),
            P(("dp", "tensor"), None),
        ),
        out_specs=(
            P(("dp", "tensor"), None),
            P(("dp", "tensor"), None),
            P(None, "dp", None, "tensor"),
            P(None, "tensor", "dp"),
            P(None, "dp", "tensor"),
            P(None, "tensor", "dp"),
            P(),
            P(),
            P(),
            P(),
        ),
        check_vma=False,
    )
```

time: 762 us -> 437 us (0.57)
  waiting for transfers between devices: 383 us -> 0 us
  Pallas kernels: 0 us -> 271 us
  blocking collectives: 148 us -> 0 us
  starting transfers between devices: 66.8 us -> 0 us
  local copies, waits for them, and re-layouts: 27.6 us -> 58.1 us
  between operations: 16.3 us -> 1.08 us
  other arithmetic: 39 us -> 27.5 us
    reduce_scatter x7 -> x0, waiting for transfers between devices: 275 us -> none  [the longest x1 72.5 us: layer_backward(): lax.psum_scatter(up_grad, 'dp', scatter_dimension=0, tiled=True)]
    pallas_call x0 -> x6, Pallas kernels: none -> 271 us  [call(): pl.pallas_call(partial(kernel, sizes), out_shape=[jax.ShapeDtypeStruct(s,...]
    all_gather x6 -> x0, blocking collectives: 106 us -> none  [the longest x1 38 us: shards(): lax.all_gather(qkv_weight[layer_idx], 'dp', axis=0, tiled=True)]
    ppermute x24 -> x0, starting transfers between devices: 66.4 us -> none  [passed_along(): lax.ppermute(value, axis, [(source, source + steps) for source in range(i...]
    all_gather x2 -> x0, waiting for transfers between devices: 41.6 us -> none  [the longest x1 35.7 us: shards(): lax.all_gather(down_weight[layer_idx], 'dp', axis=1, tiled=True)]
    psum x1 -> x0, blocking collectives: 41.4 us -> none  [shards(): lax.psum((vector_stacks[0], vector_stacks[1], vector_stacks[2], vector_st...]
    ppermute x24 -> x0, waiting for transfers between devices: 34.9 us -> none  [passed_along(): lax.ppermute(value, axis, [(source, source + steps) for source in range(i...]
    unnamed x11 -> x0, waiting for transfers between devices: 31.4 us -> none
  transfers between devices with their start and end apart: 34 -> 0, of which waited for: 19 -> 0; matrix products, arithmetic and copies ran while one was open for 9% -> 0% of each run, Pallas kernels for 0% -> 0%
where the time goes in v1:
time: 437 us; the launch traced here: 436 us
  Pallas kernels  271 us (62%)
  matrix products  78 us (18%)
  local copies, waits for them, and re-layouts  58.1 us (13%)
  other arithmetic  27.5 us (6%)
    pallas_call x6, Pallas kernels, call(): pl.pallas_call(partial(kernel, sizes), out_shape=[jax.ShapeDtypeStruct(s,...  271 us
    convert_element_type x1, other arithmetic, attention_backward(): grad_scores = (attn_probs * (grad_probs - inner_sum)).astype(BF16)  15.3 us
    unnamed x40, local copies, waits for them, and re-layouts  14.4 us
    dot_general x1, matrix products, attention_backward(): jnp.einsum('qhd,khd->hqk', grad_heads, values.reshape(-1, heads_here, HEA...  13.9 us
    dot_general x4, matrix products, contract_cols(): lax.dot_general(left, right, (((1,), (1,)), ((), ())), preferred_element_...  11.6 us
    dot_general x1, matrix products, attention_forward(): jnp.einsum('hqk,khd->qhd', attn_probs, values.reshape(-1, heads_here, HEA...  9.6 us
    slice x3, local copies, waits for them, and re-layouts, shards(): all_keys, values = (window[:, :width], window[:, width:])  9.38 us
    dot_general x1, matrix products, attention_backward(): jnp.einsum('hqk,qhd->khd', attn_probs.astype(BF16), grad_heads, preferred...  9.29 us

profile of v1, /device:TPU:0, one launch (start us, length us, event | category | flops | bytes accessed | tf_op | source)
XLA Modules:
  0.0 435.8 jit_solution(1209490612089330267)
XLA Ops:
  7.6 59.8 %shard_map.186 = (bf16[4,128,768]{2,1,0:T(8,128)(2,1)}, bf16[4,128,768]{2,1,0:T(8,128)(2,1)}, bf16[8,96,2304]{2,1,0:T(8,128)(2,1)}) custom-call(bf16[128,768]{1,0:T(8,128)(2,1)} %frames.5, bf16[128,768]{1,0:T(8,128)(2,1)} %cot.3, bf16[96,2304]{1,0:T(8,128)(2,1)} %concatenate.23.weights, f32[1,768]{1,0:T(1,128)} %get-tuple-element.96.gain, ...), custom_call_target="tpu_custom_call" | custom-call | tf_op jit(solution)/shard_map/pallas_call | solution.py:363
  70.6 30.5 %shard_map.187 = bf16[7,512,384]{2,1,0:T(8,128)(2,1)} custom-call(bf16[512,384]{1,0:T(8,128)(2,1)} %slice.141.kv), custom_call_target="tpu_custom_call" | custom-call | tf_op jit(solution)/shard_map/pallas_call | solution.py:363
  101.1 4.2 fusion.35
  110.9 6.1 %fusion.38 = (f32[3,512]{1,0:T(4,128)S(1)}, f32[3,512,3584]{2,1,0:T(8,128)S(1)}) fusion(bf16[512,3,64]{0,2,1:T(8,128)(2,1)S(1)} %bitcast.119, bf16[3584,3,64]{0,2,1:T(8,128)(2,1)} %bitcast.114, pred[512,3584]{1,0:T(8,128)(4,1)} %compare_and_fusion), kind=kOutput, calls=%fused_computation.85 | convolution fusion | flops 721156608 | bytes 25434112 | tf_op jit(solution)/shard_map/qhd,khd->hqk/dot_general | solution.py:405
  117.0 3.9 fusion
  120.9 3.4 copy-done.2
  127.0 9.6 %fusion.22 = bf16[3,64,512]{2,1,0:T(8,128)(2,1)S(1)} fusion(bf16[3584,3,64]{0,2,1:T(8,128)(2,1)S(1)} %bitcast.116, f32[3,512,3584]{2,1,0:T(8,128)} %copy-done.2, f32[3,512]{1,0:T(4,128)S(1)} %fusion, f32[3,512]{1,0:T(4,128)S(1)} %get-tuple-element.88), kind=kOutput, calls=%fused_computation.43 | convolution fusion | flops 721256448 | bytes 23605248 | tf_op jit(solution)/shard_map/hqk,khd->qhd/dot_general | solution.py:423
  139.2 22.6 %shard_map.188 = (f32[128,768]{1,0:T(8,128)}, bf16[4,128,768]{2,1,0:T(8,128)(2,1)}) custom-call(bf16[4,128,768]{2,1,0:T(8,128)(2,1)} %bitcast.123, bf16[128,768]{1,0:T(8,128)(2,1)} %frames.5, f32[1,768]{1,0:T(1,128)} %get-tuple-element.97.gain, f32[1,768]{1,0:T(1,128)} %get-tuple-element.82.shift, f32[1,768]{1,0:T(1,128)} %get-tuple-element.81.bias), custom_call_target="tpu_custom_call" | custom-call | tf_op jit(solution)/shard_map/pallas_call | solution.py:363
  161.9 3.4 multiply_convert_fusion.1
  165.3 3.3 convert_reduce_fusion
  168.9 3.1 convolution_convert_fusion.1
  172.0 3.1 convolution_convert_fusion.3
  175.1 3.0 convolution_convert_fusion.4
  178.1 30.7 %shard_map.189 = (bf16[128,768]{1,0:T(8,128)(2,1)}, f32[128,768]{1,0:T(8,128)}, bf16[4,128,768]{2,1,0:T(8,128)(2,1)}, f32[4,768]{1,0:T(4,128)}) custom-call(bf16[4,128,768]{2,1,0:T(8,128)(2,1)} %bitcast.130, bf16[4,128,768]{2,1,0:T(8,128)(2,1)} %bitcast.129, f32[128,768]{1,0:T(8,128)} %get-tuple-element.28.hidden, bf16[128,768]{1,0:T(8,128)(2,1)} %cot.3, ...), custom_call_target="tpu_custom_call" | custom-call | tf_op jit(solution)/shard_map/pallas_call | solution.py:363
  214.9 6.0 %concatenate.26.grads = bf16[8,96,1728]{2,1,0:T(8,128)(2,1)} concatenate(bf16[8,96,192]{2,1,0:T(8,128)(2,1)S(1)} %convolution_convert_fusion.7, bf16[8,96,768]{2,1,0:T(8,128)(2,1)} %convolution_convert_fusion.1, bf16[8,96,768]{2,1,0:T(8,128)(2,1)} %convolution_convert_fusion), dimensions={2} | concatenate | bytes 5308416 | tf_op jit(solution)/shard_map/concatenate | solution.py:556
  222.6 13.9 %multiply_reduce_fusion = (f32[3,512]{1,0:T(4,128)S(1)}, f32[3,512,3584]{2,1,0:T(8,128)}) fusion(f32[3,512,3584]{2,1,0:T(8,128)} %copy-done.2, f32[3,512]{1,0:T(4,128)S(1)} %log_add_fusion, bf16[512,3,64]{0,2,1:T(8,128)(2,1)S(1)} %bitcast.125, bf16[3584,3,64]{0,2,1:T(8,128)(2,1)S(1)} %bitcast.117), kind=kOutput, calls=%fused_computation.1 | convolution fusion | flops 721156608 | bytes 45625344 | tf_op jit(solution)/shard_map/qhd,khd->hqk/dot_general | solution.py:438
  236.5 15.3 %multiply_convert_fusion = bf16[3,512,3584]{2,1,0:T(8,128)(2,1)S(1)} fusion(f32[3,512,3584]{2,1,0:T(8,128)} %get-tuple-element.93, f32[3,512,3584]{2,1,0:T(8,128)} %copy-done.2, f32[3,512]{1,0:T(4,128)S(1)} %get-tuple-element.92, f32[3,512]{1,0:T(4,128)S(1)} %log_add_fusion), kind=kLoop, calls=%fused_computation | loop fusion | flops 22020096 | bytes 55062528 | tf_op jit(solution)/shard_map/convert_element_type | solution.py:443
  251.8 4.0 copy-done.3
  263.2 9.3 %fusion.11 = bf16[3584,3,64]{0,2,1:T(8,128)(2,1)S(1)} fusion(bf16[512,3,64]{0,2,1:T(8,128)(2,1)S(1)} %bitcast.126, f32[3,512,3584]{2,1,0:T(8,128)} %copy-done.2, f32[3,512]{1,0:T(4,128)S(1)} %log_add_fusion), kind=kOutput, calls=%fused_computation.16 | convolution fusion | flops 716341248 | bytes 23599104 | tf_op jit(solution)/shard_map/hqk,qhd->khd/dot_general | solution.py:452
  275.0 4.1 copy.62
  279.1 4.0 pad_maximum_fusion.dkv
  283.1 97.6 %shard_map.190 = (f32[512,384]{1,0:T(8,128)}, f32[96,1728]{1,0:T(8,128)}) custom-call(bf16[7,512,384]{2,1,0:T(8,128)(2,1)} %pad_maximum_fusion.dkv, bf16[8,96,1728]{2,1,0:T(8,128)(2,1)} %concatenate.26.grads), custom_call_target="tpu_custom_call" | custom-call | tf_op jit(solution)/shard_map/pallas_call | solution.py:363
  381.9 7.6 %fusion.21 = bf16[3,64,512]{2,1,0:T(8,128)(2,1)S(1)} fusion(bf16[3584,3,64]{0,2,1:T(8,128)(2,1)S(1)} %bitcast.115, bf16[3,512,3584]{2,1,0:T(8,128)(2,1)} %copy-done.3), kind=kOutput, calls=%fused_computation.41 | convolution fusion | flops 704839680 | bytes 12582912 | tf_op jit(solution)/shard_map/hqk,khd->qhd/dot_general | solution.py:444
  397.4 29.7 %shard_map.191 = (bf16[128,768]{1,0:T(8,128)(2,1)}, f32[96,576]{1,0:T(8,128)}, f32[16,768]{1,0:T(8,128)}) custom-call(bf16[4,128,768]{2,1,0:T(8,128)(2,1)} %bitcast.131, bf16[128,768]{1,0:T(8,128)(2,1)} %frames.5, f32[128,768]{1,0:T(8,128)} %get-tuple-element.32.dh, f32[1,768]{1,0:T(1,128)} %get-tuple-element.96.gain, bf16[8,96,576]{2,1,0:T(8,128)(2,1)} %bitcast.118, ...), custom_call_target="tpu_custom_call" | custom-call | tf_op jit(solution)/shard_map/pallas_call | solution.py:363
  (95 shorter events, 56.4 us)
Async XLA Ops:
  0.6 161.2 %copy-start = (f32[1,3072]{1,0:T(1,128)S(1)}, f32[1,3072]{1,0:T(1,128)}, u32[]{:S(2)}) copy-start(f32[1,3072]{1,0:T(1,128)} %param.20) | copy-start | bytes 36868
  105.3 2.6 copy-start.12
  117.0 7.3 %copy-start.2 = (f32[3,512,3584]{2,1,0:T(8,128)}, f32[3,512,3584]{2,1,0:T(8,128)S(1)}, u32[]{:S(2)}) copy-start(f32[3,512,3584]{2,1,0:T(8,128)S(1)} %get-tuple-element.89) | copy-start | bytes 66060292
  161.9 3.4 copy-start.6
  165.3 3.3 copy-start.7
  168.9 3.1 copy-start.15
  172.0 3.1 copy-start.14
  214.9 6.0 %copy-start.5 = (bf16[4,128,768]{2,1,0:T(8,128)(2,1)S(1)}, bf16[4,128,768]{2,1,0:T(8,128)(2,1)}, u32[]{:S(2)}) copy-start(bf16[4,128,768]{2,1,0:T(8,128)(2,1)} %get-tuple-element.30) | copy-start | bytes 2359300
  251.8 4.0 copy-start.3
  283.1 98.8 %copy-start.4 = (bf16[3584,192]{0,1:T(8,128)(2,1)S(1)}, bf16[3584,192]{0,1:T(8,128)(2,1)}, u32[]{:S(2)}) copy-start(bf16[3584,192]{0,1:T(8,128)(2,1)} %copy.60) | copy-start | bytes 4128772
  381.9 8.7 %copy-start.11 = (f32[4,768]{1,0:T(4,128)S(1)}, f32[4,768]{1,0:T(4,128)}, u32[]{:S(2)}) copy-start(f32[4,768]{1,0:T(4,128)} %get-tuple-element.33) | copy-start | bytes 36868
  381.9 10.3 %copy-start.13 = (bf16[4,128,768]{2,1,0:T(8,128)(2,1)S(1)}, bf16[4,128,768]{2,1,0:T(8,128)(2,1)}, u32[]{:S(2)}) copy-start(bf16[4,128,768]{2,1,0:T(8,128)(2,1)} %get-tuple-element.24) | copy-start | bytes 2359300
  397.4 35.2 %copy-start.8 = (f32[96,1728]{1,0:T(8,128)S(1)}, f32[96,1728]{1,0:T(8,128)}, u32[]{:S(2)}) copy-start(f32[96,1728]{1,0:T(8,128)} %get-tuple-element.36) | copy-start | bytes 1990660
  397.4 38.3 %copy-start.1 = (f32[1,3072]{1,0:T(1,128)S(1)}, f32[1,3072]{1,0:T(1,128)}, u32[]{:S(2)}) copy-start(f32[1,3072]{1,0:T(1,128)} %param.20) | copy-start | bytes 36868
  427.2 7.2 %copy-start.9 = (bf16[128,768]{1,0:T(8,128)(2,1)S(1)}, bf16[128,768]{1,0:T(8,128)(2,1)}, u32[]{:S(2)}) copy-start(bf16[128,768]{1,0:T(8,128)(2,1)} %get-tuple-element.110) | copy-start | bytes 589828
  427.2 7.9 %copy-start.10 = (bf16[128,768]{1,0:T(8,128)(2,1)S(1)}, bf16[128,768]{1,0:T(8,128)(2,1)}, u32[]{:S(2)}) copy-start(bf16[128,768]{1,0:T(8,128)(2,1)} %get-tuple-element.111) | copy-start | bytes 589828

commit v2 on v1

--- a/solution.py
+++ b/solution.py
@@ -113,13 +113,17 @@
     return direct, forwards
 
 
-def gather_finish(place, full, direct, forwards, xs, xr):
+def forward_on(place, full, direct, forwards, xs, xr):
     for k in range(1, place.half):
         direct[k].wait_recv()
         got = full.at[place.hi_back(k) * 2 + place.lo]
         c = send(got, got, xs.at[k], xr.at[k], place.partner())
         c.start()
         forwards.append(c)
+
+
+def gather_finish(place, full, direct, forwards, xs, xr):
+    forward_on(place, full, direct, forwards, xs, xr)
     for k in range(1, place.half):
         direct[k].wait_send()
     for c in forwards:
@@ -177,56 +181,101 @@
     return jnp.sum(values, axis=0, keepdims=True)
 
 
-def open_kernel(sizes, frames, cot, weights, gain, shift, normed_g, cot_g, w_full,
-                mine, ns, nr, cs, cr, ws, wr, xs, xr):
+def open_kernel(sizes, frames, weights, gain, shift, normed_g, w_full,
+                mine, ns, nr, ws, wr, xs, xr):
     place = Place(sizes)
     greet(tensor_peers(place) + two_level_peers(place))
     direct, forwards = gather_start(place, weights, w_full, ws, wr, xs, xr)
-    cots = tensor_gather_start(place, cot, cot_g, cs, cr)
     xhat, _ = norm_parts(frames[...].astype(F32))
     mine[...] = (xhat * gain[...] + shift[...]).astype(BF16)
     normeds = tensor_gather_start(place, mine, normed_g, ns, nr)
     normed_g[place.t] = mine[...]
-    cot_g[place.t] = cot[...]
     w_full[place.dp] = weights[...]
     gather_finish(place, w_full, direct, forwards, xs, xr)
-    for c in cots + normeds:
+    for c in normeds:
         c.wait()
 
 
-def near_kernel(sizes, kv, window, ss, rs):
-    place = Place(sizes)
-    n = place.n
-    gaps = [g for g in (1, -1, 2, -2, 3, -3)]
+GAPS = (1, -1, 2, -2, 3, -3)
+
+
+def inside(place, g):
+    return (place.dp + g >= 0) & (place.dp + g < place.n)
+
+
+def greet_near(place, peers):
     barrier = pltpu.get_barrier_semaphore()
-    here = [(place.dp + g >= 0) & (place.dp + g < n) for g in gaps]
-    for g, ok in zip(gaps, here):
-        @pl.when(ok)
+    for peer in peers:
+        pl.semaphore_signal(barrier, inc=1, device_id=peer, device_id_type=MESH)
+    for g in GAPS:
+        @pl.when(inside(place, g))
         def _(g=g):
             pl.semaphore_signal(barrier, inc=1, device_id={"dp": place.dp + g},
                                 device_id_type=MESH)
-    pl.semaphore_wait(barrier, sum(ok.astype(jnp.int32) for ok in here))
+    pl.semaphore_wait(
+        barrier, len(peers) + sum(inside(place, g).astype(jnp.int32) for g in GAPS)
+    )
+
+
+def dot(left, right, dims):
+    return lax.dot_general(left, right, ((dims[:1], dims[1:]), ((), ())),
+                           preferred_element_type=F32)
+
+
+def attend_kernel(sizes, queries, kv, qid, kid, cot, weights,
+                  attended, lse, window, cot_g, w_full,
+                  ks, kr, cs, cr, ws, wr, xs, xr):
+    place = Place(sizes)
+    greet_near(place, tensor_peers(place) + two_level_peers(place))
 
     def copy(i, g):
-        return send(kv, window.at[REACH - g], ss.at[i], rs.at[i], {"dp": place.dp + g})
-
-    for i, g in enumerate(gaps):
-        @pl.when(here[i])
+        return send(kv, window.at[REACH - g], ks.at[i], kr.at[i], {"dp": place.dp + g})
+
+    for i, g in enumerate(GAPS):
+        @pl.when(inside(place, g))
         def _(i=i, g=g):
             copy(i, g).start()
+    direct, forwards = gather_start(place, weights, w_full, ws, wr, xs, xr)
+    cots = tensor_gather_start(place, cot, cot_g, cs, cr)
     window[REACH] = kv[...]
-    for i, g in enumerate(gaps):
-        @pl.when(jnp.logical_not((place.dp - g >= 0) & (place.dp - g < n)))
+    cot_g[place.t] = cot[...]
+    w_full[place.dp] = weights[...]
+    for i, g in enumerate(GAPS):
+        @pl.when(jnp.logical_not(inside(place, -g)))
         def _(g=g):
             window[REACH - g] = jnp.zeros_like(kv)
-    for i, g in enumerate(gaps):
-        @pl.when(here[i])
+    for i, g in enumerate(GAPS):
+        @pl.when(inside(place, g))
         def _(i=i, g=g):
             copy(i, g).wait_send()
 
-        @pl.when((place.dp - g >= 0) & (place.dp - g < n))
+        @pl.when(inside(place, -g))
         def _(i=i, g=g):
             copy(i, g).wait_recv()
+    width = queries.shape[1]
+    count = kid.shape[0]
+    step = min(256, queries.shape[0])
+    for h in range(width // HEAD):
+        cols = slice(h * HEAD, (h + 1) * HEAD)
+        vcols = slice(width + h * HEAD, width + (h + 1) * HEAD)
+        for first in range(0, queries.shape[0], step):
+            rows = slice(first, first + step)
+            keys = window[:, :, cols].reshape(count, HEAD)
+            values = window[:, :, vcols].reshape(count, HEAD)
+            scores = dot(keys, queries[rows, cols], (1, 1)) * HEAD ** (-0.5)
+            scores = jnp.where(kid[...] == qid[:, rows], scores, -1000000000.0)
+            largest = jnp.max(scores, axis=0, keepdims=True)
+            exps = jnp.exp(scores - largest)
+            totals = jnp.sum(exps, axis=0, keepdims=True)
+            probs = (exps * (1.0 / totals)).astype(BF16)
+            lse[h:h + 1, rows] = largest + jnp.log(totals)
+            attended[rows, cols] = dot(values, probs, (0, 0)).T.astype(BF16)
+        if h == 0:
+            forward_on(place, w_full, direct, forwards, xs, xr)
+    for k in range(1, place.half):
+        direct[k].wait_send()
+    for c in forwards + cots:
+        c.wait()
 
 
 def middle_kernel(sizes, part, frames, gain, shift, bias, hidden, c_g,
@@ -244,10 +293,12 @@
         c.wait()
 
 
-def turn_kernel(sizes, down, dc_part, hidden, cot, gain, bias, encoded, dh_out, dz_g, vec,
-                slots_d, slots_c, mine, ds, dr, cs, cr, zs, zr):
+def turn_kernel(sizes, down, dc_part, hidden, cot, gain, bias, grads,
+                encoded, dh_out, dz_g, vec, halves,
+                slots_d, slots_c, mine, rx, ds, dr, cs, cr, zs, zr, xs, xr):
     place = Place(sizes)
-    greet(tensor_peers(place))
+    greet(tensor_peers(place) + [place.partner()])
+    x_copies = scatter_start(place, grads, rx, xs, xr)
     c_copies = tensor_scatter_start(place, dc_part, slots_c, cs, cr)
     d_copies = tensor_scatter_start(place, down, slots_d, ds, dr)
     h = hidden[...]
@@ -266,50 +317,93 @@
     encoded[...] = (
         h + (tensor_scatter_sum(place, down, slots_d, d_copies) + bias[...])
     ).astype(BF16)
+    for k in list(range(1, place.half)) + [0]:
+        x_copies[k].wait()
+        halves[k] = (
+            grads[place.hi_at(k) * 2 + place.lo].astype(F32) + rx[k].astype(F32)
+        ).astype(BF16)
     for c in sends:
         c.wait()
 
 
-def back_kernel(sizes, dkv, grads, dkv_out, grads_out,
-                slots, rx, stage, rz, ks, kr, xs, xr, ss, rs):
+def back_kernel(sizes, queries, window, grad_out, lse, qid, kid, mlp, outs,
+                dq, dkv_out, mlp_out, outs_out,
+                probs, gprobs, dqt, dkv, slots, mz, rx, stage, rz,
+                ks, kr, ms, mr, xs, xr, ss, rs):
     place = Place(sizes)
-    n = place.n
-    gaps = [g for g in (1, -1, 2, -2, 3, -3)]
-
-    def inside(g):
-        return (place.dp + g >= 0) & (place.dp + g < n)
-
-    peers = two_level_peers(place)
-    barrier = pltpu.get_barrier_semaphore()
-    for peer in peers:
-        pl.semaphore_signal(barrier, inc=1, device_id=peer, device_id_type=MESH)
-    for g in gaps:
-        @pl.when(inside(g))
-        def _(g=g):
-            pl.semaphore_signal(barrier, inc=1, device_id={"dp": place.dp + g},
-                                device_id_type=MESH)
-    pl.semaphore_wait(barrier, len(peers) + sum(inside(g).astype(jnp.int32) for g in gaps))
+    greet_near(place, two_level_peers(place))
+    copies = scatter_start(place, outs, rx, xs, xr)
+    m_copies = [None]
+    for k in range(1, place.half):
+        c = send(mlp.at[k], mz.at[k], ms.at[k], mr.at[k], place.along(k))
+        c.start()
+        m_copies.append(c)
 
     def copy(i, g):
         return send(dkv.at[REACH + g], slots.at[i], ks.at[i], kr.at[i], {"dp": place.dp + g})
 
-    for i, g in enumerate(gaps):
-        @pl.when(inside(g))
-        def _(i=i, g=g):
-            copy(i, g).start()
-    copies = scatter_start(place, grads, rx, xs, xr)
+    width = queries.shape[1]
+    heads = width // HEAD
+    blocks, group = window.shape[0], window.shape[1]
+    scale = HEAD ** (-0.5)
+    order = [3, -3, 2, -2, 1, -1, 0]
+    onward = None
+    for h in range(heads):
+        cols = slice(h * HEAD, (h + 1) * HEAD)
+        vcols = slice(width + h * HEAD, width + (h + 1) * HEAD)
+
+        def first(d, inner, h=h, cols=cols, vcols=vcols):
+            scores = dot(window[d, :, cols], queries[:, cols], (1, 1)) * scale
+            p = jnp.exp(jnp.where(kid[d] == qid[...], scores, -1000000000.0) - lse[h:h + 1])
+            gp = dot(window[d, :, vcols], grad_out[:, cols], (1, 1))
+            probs[d] = p
+            gprobs[d] = gp
+            return inner + jnp.sum(p * gp, axis=0, keepdims=True)
+
+        inner = lax.fori_loop(0, blocks, first, jnp.zeros((1, group), F32))
+        dqt[...] = jnp.zeros_like(dqt)
+
+        def second(d, cols=cols, vcols=vcols, inner=inner):
+            p = probs[d]
+            ds = (p * (gprobs[d] - inner)).astype(BF16)
+            dqt[...] += dot(window[d, :, cols], ds, (0, 0))
+            dkv[d, :, cols] = (dot(ds, queries[:, cols], (1, 0)) * scale).astype(BF16)
+            dkv[d, :, vcols] = dot(p.astype(BF16), grad_out[:, cols], (1, 0)).astype(BF16)
+
+        if h < heads - 1:
+            def step(d, carry, second=second):
+                second(d)
+                return carry
+
+            lax.fori_loop(0, blocks, step, 0)
+        else:
+            for g in order:
+                second(REACH + g)
+                if g:
+                    @pl.when(inside(place, g))
+                    def _(g=g):
+                        copy(GAPS.index(g), g).start()
+        dq[:, cols] = (dqt[...].T * scale).astype(BF16)
+        if h == 0:
+            onward = scatter_middle(place, outs, rx, stage, rz, copies, ss, rs)
     dkv_out[...] = dkv[REACH].astype(F32)
-    onward = scatter_middle(place, grads, rx, stage, rz, copies, ss, rs)
-    for i, g in enumerate(gaps):
-        @pl.when(inside(g))
+    scatter_finish(place, outs, rx, rz, onward, outs_out)
+    total = mlp[0].astype(F32)
+    for k in range(1, place.half):
+        m_copies[k].wait()
+        total = total + mz[k].astype(F32)
+    mlp_out[...] = total
+    for g in order[:-1]:
+        i = GAPS.index(g)
+
+        @pl.when(inside(place, g))
         def _(i=i, g=g):
             copy(i, g).wait_send()
 
-        @pl.when(inside(-g))
+        @pl.when(inside(place, -g))
         def _(i=i, g=g):
             copy(i, g).wait_recv()
             dkv_out[...] += slots[i].astype(F32)
-    scatter_finish(place, grads, rx, rz, onward, grads_out)
 
 
 def close_kernel(sizes, da_part, frames, dh, gain, grads, vec_in, frames_grad, grads_out, vec_out,
@@ -388,77 +482,6 @@
     )
 
 
-def attention_mask(dp_idx, dp_count, group_rows, clip_offsets):
-    window = (2 * REACH + 1) * group_rows
-    query_pos = dp_idx * group_rows + jnp.arange(group_rows, dtype=jnp.int32)
-    key_pos = (dp_idx - REACH) * group_rows + jnp.arange(window, dtype=jnp.int32)
-    inside = (key_pos >= 0) & (key_pos < dp_count * group_rows)
-    same_clip = (
-        clip_ids(query_pos, clip_offsets)[:, None] == clip_ids(key_pos, clip_offsets)[None, :]
-    )
-    return same_clip & inside[None, :]
-
-
-def head_scores(queries, all_keys, allowed):
-    group_rows = queries.shape[0]
-    heads_here = queries.shape[1] // HEAD
-    scores = jnp.einsum(
-        "qhd,khd->hqk",
-        queries.reshape(group_rows, heads_here, HEAD),
-        all_keys.reshape(all_keys.shape[0], heads_here, HEAD),
-        preferred_element_type=jnp.float32,
-    ) * HEAD ** (-0.5)
-    return jnp.where(allowed[None], scores, -1000000000.0)
-
-
-def attention_forward(queries, all_keys, values, allowed):
-    group_rows, local_width = queries.shape
-    heads_here = local_width // HEAD
-    masked = head_scores(queries, all_keys, allowed)
-    largest = jnp.max(masked, axis=-1, keepdims=True)
-    weights = jnp.exp(masked - largest)
-    totals = jnp.sum(weights, axis=-1, keepdims=True)
-    attn_probs = (weights / totals).astype(BF16)
-    log_total = largest + jnp.log(totals)
-    attended = jnp.einsum(
-        "hqk,khd->qhd", attn_probs, values.reshape(-1, heads_here, HEAD),
-        preferred_element_type=F32,
-    )
-    return log_total, attended.reshape(group_rows, local_width).astype(BF16)
-
-
-def attention_backward(grad_attended, queries, all_keys, values, allowed, log_total):
-    group_rows = queries.shape[0]
-    local_width = queries.shape[1]
-    heads_here = local_width // HEAD
-    head_scale = HEAD ** (-0.5)
-    masked = head_scores(queries, all_keys, allowed)
-    attn_probs = jnp.exp(masked - log_total)
-    grad_heads = grad_attended.reshape(group_rows, heads_here, HEAD)
-    grad_probs = jnp.einsum(
-        "qhd,khd->hqk", grad_heads, values.reshape(-1, heads_here, HEAD),
-        preferred_element_type=F32,
-    )
-    inner_sum = jnp.sum(attn_probs * grad_probs, axis=-1, keepdims=True)
-    grad_scores = (attn_probs * (grad_probs - inner_sum)).astype(BF16)
-    grad_queries = jnp.einsum(
-        "hqk,khd->qhd", grad_scores, all_keys.reshape(-1, heads_here, HEAD),
-        preferred_element_type=F32,
-    ) * head_scale
-    grad_keys = jnp.einsum(
-        "hqk,qhd->khd", grad_scores, queries.reshape(group_rows, heads_here, HEAD),
-        preferred_element_type=F32,
-    ) * head_scale
-    grad_values = jnp.einsum(
-        "hqk,qhd->khd", attn_probs.astype(BF16), grad_heads, preferred_element_type=F32,
-    )
-    shape = (2 * REACH + 1, group_rows, local_width)
-    dkv = jnp.concatenate(
-        [grad_keys.astype(BF16).reshape(shape), grad_values.astype(BF16).reshape(shape)], axis=2
-    )
-    return grad_queries.reshape(group_rows, local_width).astype(BF16), dkv
-
-
 def place_slice(piece, tensor_idx, full_width):
     return lax.dynamic_update_slice_in_dim(
         jnp.zeros((full_width,), F32), piece, tensor_idx * piece.shape[0], 0
@@ -483,41 +506,45 @@
     ff_all = fc_bias.shape[1]
     gains, shifts, pbias, fbias = ln_gain[0], ln_bias[0], proj_bias[0], fc_bias[0]
 
-    w_local = jnp.concatenate(
-        [qkv_weight[0].reshape(wrows, 3 * width), out_weight[0].T, up_weight[0], down_weight[0].T],
-        axis=1,
-    )
+    w_local = jnp.concatenate([out_weight[0].T, up_weight[0], down_weight[0].T], axis=1)
+    w_qkv = qkv_weight[0].reshape(wrows, 3 * width)
     total = w_local.shape[1]
     t3 = (t_count, rows, D)
-    normed_g, cot_g, w_full = call(
+    normed_g, qkv_full = call(
         open_kernel, sizes, 1,
-        [(t3, BF16), (t3, BF16), ((n, wrows, total), BF16)],
-        [pltpu.VMEM((rows, D), BF16), dma(t_count), dma(t_count), dma(t_count), dma(t_count),
+        [(t3, BF16), ((n, wrows, 3 * width), BF16)],
+        [pltpu.VMEM((rows, D), BF16), dma(t_count), dma(t_count),
          dma(half), dma(half), dma(half), dma(half)],
-        frames, out_cotangent, w_local, gains[0:1], shifts[0:1],
+        frames, w_qkv, gains[0:1], shifts[0:1],
     )
     normed_g = normed_g.reshape(group, D)
-    cot_g = cot_g.reshape(group, D)
-    w_full = w_full.reshape(D, total)
-    cut = [3 * width, 4 * width, 4 * width + ff]
-    qkv_full = w_full[:, :cut[0]]
-    out_t = w_full[:, cut[0]:cut[1]]
-    up_full = w_full[:, cut[1]:cut[2]]
-    down_t = w_full[:, cut[2]:]
-
-    allowed = attention_mask(dp_idx, n, group, clip_offsets)
+    qkv_full = qkv_full.reshape(D, 3 * width)
+
     q_bias = lax.dynamic_slice_in_dim(pbias[0], t_idx * width, width)
     v_bias = lax.dynamic_slice_in_dim(pbias[1], t_idx * width, width)
     bias_row = jnp.concatenate([q_bias, jnp.zeros_like(q_bias), v_bias])
     projected = (jnp.dot(normed_g, qkv_full, preferred_element_type=F32) + bias_row).astype(BF16)
     queries = projected[:, :width]
-    (window,) = call(
-        near_kernel, sizes, 2, [((2 * REACH + 1, group, 2 * width), BF16)],
-        [dma(6), dma(6)], projected[:, width:],
-    )
-    window = window.reshape(-1, 2 * width)
-    all_keys, values = window[:, :width], window[:, width:]
-    log_total, attended = attention_forward(queries, all_keys, values, allowed)
+    blocks = 2 * REACH + 1
+    query_pos = dp_idx * group + jnp.arange(group, dtype=jnp.int32)
+    key_pos = (dp_idx - REACH) * group + jnp.arange(blocks * group, dtype=jnp.int32)
+    qid = clip_ids(query_pos, clip_offsets)[None]
+    kid = jnp.where(
+        (key_pos >= 0) & (key_pos < n * group), clip_ids(key_pos, clip_offsets), -2
+    )[:, None]
+    heads = width // HEAD
+    attended, lse, window, cot_g, w_full = call(
+        attend_kernel, sizes, 2,
+        [((group, width), BF16), ((heads, group), F32), ((blocks, group, 2 * width), BF16),
+         (t3, BF16), ((n, wrows, total), BF16)],
+        [dma(6), dma(6), dma(t_count), dma(t_count), dma(half), dma(half), dma(half), dma(half)],
+        queries, projected[:, width:], qid, kid, out_cotangent, w_local,
+    )
+    cot_g = cot_g.reshape(group, D)
+    w_full = w_full.reshape(D, total)
+    out_t = w_full[:, :width]
+    up_full = w_full[:, width:width + ff]
+    down_t = w_full[:, width + ff:]
 
     part = contract_cols(attended, out_t).astype(BF16).reshape(t3)
     hidden, c_g = call(
@@ -537,33 +564,35 @@
     grad_act = jnp.dot(cot_g, down_t, preferred_element_type=F32)
     grad_upper = (grad_act * slope).astype(BF16)
     dc_part = contract_cols(grad_upper, up_full).astype(BF16).reshape(t3)
-    encoded, dh, dz_g, vec2 = call(
+    down_grad_t = contract_rows(cot_g, activated)
+    up_grad = contract_rows(c_g, grad_upper)
+    mlp = jnp.concatenate([up_grad, down_grad_t], axis=1).astype(BF16).reshape(n, wrows, 2 * ff)
+    mlp_blocks = pltpu.VMEM((half, wrows, 2 * ff), BF16)
+    encoded, dh, dz_g, vec2, mlp = call(
         turn_kernel, sizes, 4,
-        [((rows, D), BF16), ((rows, D), F32), (t3, BF16), ((4, D), F32)],
+        [((rows, D), BF16), ((rows, D), F32), (t3, BF16), ((4, D), F32),
+         ((half, wrows, 2 * ff), BF16)],
         [pltpu.VMEM((t_count - 1, rows, D), BF16), pltpu.VMEM((t_count - 1, rows, D), BF16),
-         pltpu.VMEM((rows, D), BF16)] + [dma(t_count)] * 6,
-        down_part, dc_part, hidden, out_cotangent, gains[1:2], pbias[3:4],
+         pltpu.VMEM((rows, D), BF16), mlp_blocks] + [dma(t_count)] * 6 + [dma(half)] * 2,
+        down_part, dc_part, hidden, out_cotangent, gains[1:2], pbias[3:4], mlp,
     )
     dz_g = dz_g.reshape(group, D)
     fc_grad = place_slice(jnp.sum(grad_upper, axis=0, dtype=F32), t_idx, ff_all)
-    down_grad_t = contract_rows(cot_g, activated)
-    up_grad = contract_rows(c_g, grad_upper)
-    out_grad_t = contract_rows(dz_g, attended)
+    outs = contract_rows(dz_g, attended).astype(BF16).reshape(n, wrows, width)
     grad_attended = jnp.dot(dz_g, out_t, preferred_element_type=F32).astype(BF16)
-    grad_queries, dkv = attention_backward(
-        grad_attended, queries, all_keys, values, allowed, log_total
-    )
-    three = jnp.concatenate([out_grad_t, up_grad, down_grad_t], axis=1).astype(BF16)
-    w3 = three.shape[1]
-    dkv_sum, three = call(
-        back_kernel, sizes, 5, [((group, 2 * width), F32), ((wrows, w3), F32)],
-        [pltpu.VMEM((6, group, 2 * width), BF16)] + [pltpu.VMEM((half, wrows, w3), BF16)] * 3
-        + [dma(6)] * 2 + [dma(half)] * 4,
-        dkv, three.reshape(n, wrows, w3),
-    )
-    out_grad = three[:, :width].T
-    up_grad = three[:, width:width + ff]
-    down_grad = three[:, width + ff:].T
+    grad_queries, dkv_sum, mlp, out_grad = call(
+        back_kernel, sizes, 5,
+        [((group, width), BF16), ((group, 2 * width), F32), ((wrows, 2 * ff), F32),
+         ((wrows, width), F32)],
+        [pltpu.VMEM((blocks, group, group), F32)] * 2 + [pltpu.VMEM((HEAD, group), F32)]
+        + [pltpu.VMEM((blocks, group, 2 * width), BF16), pltpu.VMEM((6, group, 2 * width), BF16)]
+        + [mlp_blocks] + [pltpu.VMEM((half, wrows, width), BF16)] * 3
+        + [dma(6)] * 2 + [dma(half)] * 6,
+        queries, window, grad_attended, lse, qid, kid.reshape(blocks, group, 1), mlp, outs,
+    )
+    out_grad = out_grad.T
+    up_grad = mlp[:, :ff]
+    down_grad = mlp[:, ff:].T
 
     grad_proj = jnp.concatenate([grad_queries, dkv_sum.astype(BF16)], axis=1)
     qkv_grad = contract_rows(normed_g, grad_proj).astype(BF16)

time: 437 us -> 331 us (0.76)
  matrix products: 78 us -> 24.9 us
  local copies, waits for them, and re-layouts: 58.1 us -> 24.8 us
  other arithmetic: 27.5 us -> 9.28 us
    dot_general x6 -> x0, matrix products: 48.6 us -> none  [the longest x1 13.9 us: attention_backward(): jnp.einsum('qhd,khd->hqk', grad_heads, values.reshape(-1, heads_here, HEA...]
    convert_element_type x1 -> x0, other arithmetic: 15.3 us -> none  [attention_backward(): grad_scores = (attn_probs * (grad_probs - inner_sum)).astype(BF16)]
    reshape x4 -> x0, local copies, waits for them, and re-layouts: 12 us -> none  [the longest x2 6.65 us: attention_backward(): grad_values.astype(BF16).reshape(shape)]
    slice x3 -> x0, local copies, waits for them, and re-layouts: 9.38 us -> none  [shards(): all_keys, values = (window[:, :width], window[:, width:])]
    unnamed x40 -> x48, local copies, waits for them, and re-layouts: 14.4 us -> 7.4 us
    concatenate x2 -> x1, local copies, waits for them, and re-layouts: 7.82 us -> 1.02 us  [shards(): jnp.concatenate([out_weight[0].T, up_weight[0], down_weight[0].T], axis=1)]
where the time goes in v2:
time: 331 us; the launch traced here: 328 us
  Pallas kernels  267 us (81%)
  matrix products  24.9 us (8%)
  local copies, waits for them, and re-layouts  24.8 us (7%)
  other arithmetic  9.28 us (3%)
    pallas_call x6, Pallas kernels, call(): pl.pallas_call(partial(kernel, sizes), out_shape=[jax.ShapeDtypeStruct(s,...  267 us
    dot_general x4, matrix products, contract_cols(): lax.dot_general(left, right, (((1,), (1,)), ((), ())), preferred_element_...  7.79 us
    unnamed x48, local copies, waits for them, and re-layouts  7.4 us

profile of v2, /device:TPU:0, one launch (start us, length us, event | category | flops | bytes accessed | tf_op | source)
XLA Modules:
  0.0 327.5 jit_solution(9387090494527853679)
XLA Ops:
  0.7 1.4 slice_bitcast_fusion.6
  2.3 1.4 slice_bitcast_fusion.8
  5.5 24.1 %shard_map.186 = (bf16[4,128,768]{2,1,0:T(8,128)(2,1)}, bf16[8,96,576]{2,1,0:T(8,128)(2,1)}) custom-call(bf16[128,768]{1,0:T(8,128)(2,1)} %frames.5, bf16[96,576]{1,0:T(8,128)(2,1)} %copy.60.weights, f32[1,768]{1,0:T(1,128)} %get-tuple-element.114.gain, f32[1,768]{1,0:T(1,128)} %get-tuple-element.105.shift), custom_call_target="tpu_custom_call" | custom-call | tf_op jit(solution)/shard_map/pallas_call | solution.py:457
  29.6 2.2 fusion.13
  33.7 2.7 reshape_select_fusion.kid
  38.3 86.3 %shard_map.187 = (bf16[512,192]{1,0:T(8,128)(2,1)}, f32[3,512]{1,0:T(4,128)}, bf16[7,512,384]{2,1,0:T(8,128)(2,1)}, bf16[4,128,768]{2,1,0:T(8,128)(2,1)}, bf16[8,96,1728]{2,1,0:T(8,128)(2,1)}) custom-call(bf16[512,192]{1,0:T(8,128)(2,1)} %slice.124.queries, bf16[512,384]{1,0:T(8,128)(2,1)} %slice.125.kv, s32[1,512]{1,0:T(1,128)} %bitcast.109, ...), custom_call_target="tpu_custom_call" | custom-call | tf_op jit(solution)/shard_map/pallas_call | solution.py:457
  124.6 2.4 convolution_convert_fusion.6
  127.0 20.3 %shard_map.188 = (f32[128,768]{1,0:T(8,128)}, bf16[4,128,768]{2,1,0:T(8,128)(2,1)}) custom-call(bf16[4,128,768]{2,1,0:T(8,128)(2,1)} %bitcast.84, bf16[128,768]{1,0:T(8,128)(2,1)} %frames.5, f32[1,768]{1,0:T(1,128)} %get-tuple-element.115.gain, f32[1,768]{1,0:T(1,128)} %get-tuple-element.104.shift, f32[1,768]{1,0:T(1,128)} %get-tuple-element.103.bias), custom_call_target="tpu_custom_call" | custom-call | tf_op jit(solution)/shard_map/pallas_call | solution.py:457
  147.3 3.6 %multiply_convert_fusion = (bf16[512,768]{1,0:T(8,128)(2,1)}, f32[512,768]{1,0:T(8,128)S(1)}) fusion(f32[768]{0:T(1024)S(1)} %dynamic-slice_reduce_fusion, bf16[512,768]{1,0:T(8,128)(2,1)} %bitcast.94, bf16[768,1728]{1,0:T(8,128)(2,1)} %bitcast.100), kind=kOutput, calls=%fused_computation.19 | convolution fusion | flops 606339072 | bytes 4328448 | tf_op jit(solution)/shard_map/dot_general | solution.py:557
  150.9 3.6 %convert_reduce_fusion = (f32[768]{0:T(1024)S(1)}, bf16[512,768]{1,0:T(8,128)(2,1)}) fusion(f32[512,768]{1,0:T(8,128)S(1)} %get-tuple-element.111, bf16[512,768]{1,0:T(8,128)(2,1)S(1)} %bitcast.92, bf16[768,1728]{1,0:T(8,128)(2,1)} %bitcast.101), kind=kOutput, calls=%fused_computation.18 | convolution fusion | flops 608697600 | bytes 4328448 | tf_op jit(solution)/shard_map/dot_general | solution.py:564
  154.8 1.9 convolution_convert_fusion.1
  157.0 1.9 convolution_convert_fusion
  159.0 1.6 pad_maximum_fusion.grads
  161.8 1.8 convolution_convert_fusion.3
  163.6 1.8 convolution_convert_fusion.4
  165.4 33.3 %shard_map.189 = (bf16[128,768]{1,0:T(8,128)(2,1)}, f32[128,768]{1,0:T(8,128)}, bf16[4,128,768]{2,1,0:T(8,128)(2,1)}, f32[4,768]{1,0:T(4,128)}, bf16[4,96,1536]{2,1,0:T(8,128)(2,1)}) custom-call(bf16[4,128,768]{2,1,0:T(8,128)(2,1)} %bitcast.90, bf16[4,128,768]{2,1,0:T(8,128)(2,1)} %bitcast.89, f32[128,768]{1,0:T(8,128)} %get-tuple-element.37.hidden, ...), custom_call_target="tpu_custom_call" | custom-call | tf_op jit(solution)/shard_map/pallas_call | solution.py:457
  198.7 1.6 convolution_convert_fusion.7
  201.2 1.4 convolution_convert_fusion.8
  203.7 1.7 sub.24
  205.4 1.6 fusion.5.kid
  207.0 55.0 %shard_map.190 = (bf16[512,192]{1,0:T(8,128)(2,1)}, f32[512,384]{1,0:T(8,128)}, f32[96,1536]{1,0:T(8,128)}, f32[96,192]{1,0:T(8,128)}) custom-call(bf16[512,192]{1,0:T(8,128)(2,1)} %slice.124.queries, bf16[7,512,384]{2,1,0:T(8,128)(2,1)} %get-tuple-element.39.window, bf16[512,192]{1,0:T(8,128)(2,1)} %copy.68.grad_out, f32[3,512]{1,0:T(4,128)} %get-tuple-element.41.lse, ...), custom_call_target="tpu_custom_call" | custom-call | tf_op jit(solution)/shard_map/pallas_call | solution.py:457
  268.9 1.8 convolution_convert_fusion.5
  270.6 48.2 %shard_map.191 = (bf16[128,768]{1,0:T(8,128)(2,1)}, f32[96,576]{1,0:T(8,128)}, f32[16,768]{1,0:T(8,128)}) custom-call(bf16[4,128,768]{2,1,0:T(8,128)(2,1)} %bitcast.91, bf16[128,768]{1,0:T(8,128)(2,1)} %frames.5, f32[128,768]{1,0:T(8,128)} %get-tuple-element.45.dh, f32[1,768]{1,0:T(1,128)} %get-tuple-element.114.gain, bf16[8,96,576]{2,1,0:T(8,128)(2,1)} %bitcast.83, ...), custom_call_target="tpu_custom_call" | custom-call | tf_op jit(solution)/shard_map/pallas_call | solution.py:457
  322.9 1.4 slice_bitcast_fusion.4
  (85 shorter events, 23.1 us)
Async XLA Ops:
  0.6 146.7 %copy-start = (f32[1,3072]{1,0:T(1,128)S(1)}, f32[1,3072]{1,0:T(1,128)}, u32[]{:S(2)}) copy-start(f32[1,3072]{1,0:T(1,128)} %param.20) | copy-start | bytes 36868
  29.6 4.0 %copy-start.15 = (s32[6]{0:T(128)S(1)}, s32[6]{0:T(128)}, u32[]{:S(2)}) copy-start(s32[6]{0:T(128)} %param.12) | copy-start | bytes 76
  31.8 5.3 %copy-start.13 = (bf16[1,192,96]{2,1,0:T(8,128)(2,1)S(1)}, bf16[1,192,96]{2,1,0:T(8,128)(2,1)}, u32[]{:S(2)}) copy-start(bf16[1,192,96]{2,1,0:T(8,128)(2,1)} %param.14) | copy-start | bytes 110596
  31.9 5.4 %copy-start.10 = (bf16[1,96,768]{2,1,0:T(8,128)(2,1)S(1)}, bf16[1,96,768]{2,1,0:T(8,128)(2,1)}, u32[]{:S(2)}) copy-start(bf16[1,96,768]{2,1,0:T(8,128)(2,1)} %param.15) | copy-start | bytes 442372
  31.9 5.4 %copy-start.11 = (bf16[1,768,96]{1,2,0:T(8,128)(2,1)S(1)}, bf16[1,768,96]{1,2,0:T(8,128)(2,1)}, u32[]{:S(2)}) copy-start(bf16[1,768,96]{1,2,0:T(8,128)(2,1)} %param.16) | copy-start | bytes 442372
  147.3 3.6 %copy-start.3 = (bf16[4,128,768]{2,1,0:T(8,128)(2,1)S(1)}, bf16[4,128,768]{2,1,0:T(8,128)(2,1)}, u32[]{:S(2)}) copy-start(bf16[4,128,768]{2,1,0:T(8,128)(2,1)} %get-tuple-element.36) | copy-start | bytes 2359300
  150.9 3.6 %copy-start.4 = (bf16[4,128,768]{2,1,0:T(8,128)(2,1)S(1)}, bf16[4,128,768]{2,1,0:T(8,128)(2,1)}, u32[]{:S(2)}) copy-start(bf16[4,128,768]{2,1,0:T(8,128)(2,1)} %get-tuple-element.35) | copy-start | bytes 2359300
  159.0 2.6 copy-start.7
  159.0 2.8 copy-start.19
  161.8 1.8 copy-start.18
  165.4 33.3 %copy-start.2 = (bf16[512,192]{1,0:T(8,128)(2,1)S(1)}, bf16[512,192]{1,0:T(8,128)(2,1)}, u32[]{:S(2)}) copy-start(bf16[512,192]{1,0:T(8,128)(2,1)} %get-tuple-element.33) | copy-start | bytes 589828
  198.7 2.5 copy-start.1
  262.0 2.9 copy-start.14
  262.1 4.5 %copy-start.6 = (bf16[512,192]{1,0:T(8,128)(2,1)S(1)}, bf16[512,192]{1,0:T(8,128)(2,1)}, u32[]{:S(2)}) copy-start(bf16[512,192]{1,0:T(8,128)(2,1)} %get-tuple-element.43) | copy-start | bytes 589828
  262.1 4.5 %copy-start.17 = (bf16[4,128,768]{2,1,0:T(8,128)(2,1)S(1)}, bf16[4,128,768]{2,1,0:T(8,128)(2,1)}, u32[]{:S(2)}) copy-start(bf16[4,128,768]{2,1,0:T(8,128)(2,1)} %get-tuple-element.31) | copy-start | bytes 2359300
  267.5 1.4 copy-start.16
  270.6 53.7 %copy-start.5 = (f32[96,1536]{1,0:T(8,128)S(1)}, f32[96,1536]{1,0:T(8,128)}, u32[]{:S(2)}) copy-start(f32[96,1536]{1,0:T(8,128)} %get-tuple-element.50) | copy-start | bytes 1769476
  318.8 6.3 %copy-start.12 = (f32[96,192]{1,0:T(8,128)S(1)}, f32[96,192]{1,0:T(8,128)}, u32[]{:S(2)}) copy-start(f32[96,192]{1,0:T(8,128)} %get-tuple-element.49) | copy-start | bytes 221188
  318.9 7.0 %copy-start.8 = (bf16[128,768]{1,0:T(8,128)(2,1)S(1)}, bf16[128,768]{1,0:T(8,128)(2,1)}, u32[]{:S(2)}) copy-start(bf16[128,768]{1,0:T(8,128)(2,1)} %get-tuple-element.128) | copy-start | bytes 589828
  318.9 7.7 %copy-start.9 = (bf16[128,768]{1,0:T(8,128)(2,1)S(1)}, bf16[128,768]{1,0:T(8,128)(2,1)}, u32[]{:S(2)}) copy-start(bf16[128,768]{1,0:T(8,128)(2,1)} %get-tuple-element.129) | copy-start | bytes 589828

commit v3 on v2

--- a/solution.py
+++ b/solution.py
@@ -222,9 +222,9 @@
                            preferred_element_type=F32)
 
 
-def attend_kernel(sizes, queries, kv, qid, kid, cot, weights,
-                  attended, lse, window, cot_g, w_full,
-                  ks, kr, cs, cr, ws, wr, xs, xr):
+def attend_kernel(sizes, queries, kv, qid, kid, cot, weights, mlp,
+                  attended, lse, window, cot_g, w_full, have, mate,
+                  ks, kr, cs, cr, ws, wr, xs, xr, ms, mr):
     place = Place(sizes)
     greet_near(place, tensor_peers(place) + two_level_peers(place))
 
@@ -252,6 +252,13 @@
         @pl.when(inside(place, -g))
         def _(i=i, g=g):
             copy(i, g).wait_recv()
+    m_copies = []
+    for k in range(1, place.half):
+        m_copies.append(send(mlp, have.at[k], ms.at[k], mr.at[k], place.along(k)))
+    m_copies.append(send(mlp, mate, ms.at[0], mr.at[0], place.partner()))
+    for c in m_copies:
+        c.start()
+    have[0] = mlp[...]
     width = queries.shape[1]
     count = kid.shape[0]
     step = min(256, queries.shape[0])
@@ -274,22 +281,31 @@
             forward_on(place, w_full, direct, forwards, xs, xr)
     for k in range(1, place.half):
         direct[k].wait_send()
-    for c in forwards + cots:
+    for c in forwards + cots + m_copies:
         c.wait()
 
 
-def middle_kernel(sizes, part, frames, gain, shift, bias, hidden, c_g,
-                  slots, mine, ps, pr, cs, cr):
+def middle_kernel(sizes, part, frames, gain, shift, bias, have, mate, hidden, c_g, mlp_full,
+                  slots, mine, ps, pr, cs, cr, xs, xr):
     place = Place(sizes)
-    greet(tensor_peers(place))
+    greet(tensor_peers(place) + [place.partner()])
     copies = tensor_scatter_start(place, part, slots, ps, pr)
+    forwards = []
+    for k in range(1, place.half):
+        c = send(have.at[k], mlp_full.at[place.hi_back(k) * 2 + place.lo], xs.at[k], xr.at[k],
+                 place.partner())
+        c.start()
+        forwards.append(c)
+    for k in range(place.half):
+        mlp_full[place.hi_back(k) * 2 + place.lo] = have[k]
+    mlp_full[place.hi * 2 + 1 - place.lo] = mate[...]
     h = frames[...].astype(F32) + (tensor_scatter_sum(place, part, slots, copies) + bias[...])
     hidden[...] = h
     xhat, _ = norm_parts(h)
     mine[...] = (xhat * gain[...] + shift[...]).astype(BF16)
     sends = tensor_gather_start(place, mine, c_g, cs, cr)
     c_g[place.t] = mine[...]
-    for c in sends:
+    for c in sends + forwards:
         c.wait()
 
 
@@ -506,9 +522,8 @@
     ff_all = fc_bias.shape[1]
     gains, shifts, pbias, fbias = ln_gain[0], ln_bias[0], proj_bias[0], fc_bias[0]
 
-    w_local = jnp.concatenate([out_weight[0].T, up_weight[0], down_weight[0].T], axis=1)
+    w_mlp = jnp.concatenate([up_weight[0], down_weight[0].T], axis=1)
     w_qkv = qkv_weight[0].reshape(wrows, 3 * width)
-    total = w_local.shape[1]
     t3 = (t_count, rows, D)
     normed_g, qkv_full = call(
         open_kernel, sizes, 1,
@@ -533,26 +548,26 @@
         (key_pos >= 0) & (key_pos < n * group), clip_ids(key_pos, clip_offsets), -2
     )[:, None]
     heads = width // HEAD
-    attended, lse, window, cot_g, w_full = call(
+    attended, lse, window, cot_g, out_t, have, mate = call(
         attend_kernel, sizes, 2,
         [((group, width), BF16), ((heads, group), F32), ((blocks, group, 2 * width), BF16),
-         (t3, BF16), ((n, wrows, total), BF16)],
-        [dma(6), dma(6), dma(t_count), dma(t_count), dma(half), dma(half), dma(half), dma(half)],
-        queries, projected[:, width:], qid, kid, out_cotangent, w_local,
+         (t3, BF16), ((n, wrows, width), BF16), ((half, wrows, 2 * ff), BF16),
+         ((wrows, 2 * ff), BF16)],
+        [dma(6), dma(6), dma(t_count), dma(t_count)] + [dma(half)] * 6,
+        queries, projected[:, width:], qid, kid, out_cotangent, out_weight[0].T, w_mlp,
     )
     cot_g = cot_g.reshape(group, D)
-    w_full = w_full.reshape(D, total)
-    out_t = w_full[:, :width]
-    up_full = w_full[:, width:width + ff]
-    down_t = w_full[:, width + ff:]
+    out_t = out_t.reshape(D, width)
 
     part = contract_cols(attended, out_t).astype(BF16).reshape(t3)
-    hidden, c_g = call(
-        middle_kernel, sizes, 3, [((rows, D), F32), (t3, BF16)],
+    hidden, c_g, mlp_full = call(
+        middle_kernel, sizes, 3, [((rows, D), F32), (t3, BF16), ((n, wrows, 2 * ff), BF16)],
         [pltpu.VMEM((t_count - 1, rows, D), BF16), pltpu.VMEM((rows, D), BF16)]
-        + [dma(t_count)] * 4,
-        part, frames, gains[1:2], shifts[1:2], pbias[2:3],
-    )
+        + [dma(t_count)] * 4 + [dma(half)] * 2,
+        part, frames, gains[1:2], shifts[1:2], pbias[2:3], have, mate,
+    )
+    mlp_full = mlp_full.reshape(D, 2 * ff)
+    up_full, down_t = mlp_full[:, :ff], mlp_full[:, ff:]
     c_g = c_g.reshape(group, D)
     upper = jnp.dot(c_g, up_full, preferred_element_type=F32)
     upper = upper + lax.dynamic_slice_in_dim(fbias, t_idx * ff, ff)

time: 331 us -> 313 us (0.946)
  Pallas kernels: 267 us -> 256 us
  matrix products: 24.9 us -> 21.2 us
    pallas_call x6, Pallas kernels: 267 us -> 256 us  [call(): pl.pallas_call(partial(kernel, sizes), out_shape=[jax.ShapeDtypeStruct(s,...]
    unnamed x48 -> x52, local copies, waits for them, and re-layouts: 7.4 us -> 6.77 us
where the time goes in v3:
time: 313 us; the launch traced here: 310 us
  Pallas kernels  256 us (82%)
  local copies, waits for them, and re-layouts  22 us (7%)
  matrix products  21.2 us (7%)
  other arithmetic  9.23 us (3%)
    pallas_call x6, Pallas kernels, call(): pl.pallas_call(partial(kernel, sizes), out_shape=[jax.ShapeDtypeStruct(s,...  256 us
    dot_general x4, matrix products, contract_cols(): lax.dot_general(left, right, (((1,), (1,)), ((), ())), preferred_element_...  8.6 us
    unnamed x52, local copies, waits for them, and re-layouts  6.77 us

profile of v3, /device:TPU:0, one launch (start us, length us, event | category | flops | bytes accessed | tf_op | source)
XLA Modules:
  0.0 309.8 jit_solution(1887510736824531443)
XLA Ops:
  3.2 1.4 slice_bitcast_fusion.8
  4.6 24.1 %shard_map.186 = (bf16[4,128,768]{2,1,0:T(8,128)(2,1)}, bf16[8,96,576]{2,1,0:T(8,128)(2,1)}) custom-call(bf16[128,768]{1,0:T(8,128)(2,1)} %frames.5, bf16[96,576]{1,0:T(8,128)(2,1)} %copy.60.weights, f32[1,768]{1,0:T(1,128)} %get-tuple-element.120.gain, f32[1,768]{1,0:T(1,128)} %get-tuple-element.111.shift), custom_call_target="tpu_custom_call" | custom-call | tf_op jit(solution)/shard_map/pallas_call | solution.py:473
  28.7 1.4 slice_bitcast_fusion.6
  30.4 2.2 fusion.13
  35.1 2.7 reshape_select_fusion.kid
  39.3 67.8 %shard_map.187 = (bf16[512,192]{1,0:T(8,128)(2,1)}, f32[3,512]{1,0:T(4,128)}, bf16[7,512,384]{2,1,0:T(8,128)(2,1)}, bf16[4,128,768]{2,1,0:T(8,128)(2,1)}, bf16[8...) custom-call(bf16[512,192]{1,0:T(8,128)(2,1)} %slice.120.queries, ...), custom_call_target="tpu_custom_call" | custom-call | tf_op jit(solution)/shard_map/pallas_call | solution.py:473
  107.1 2.4 convolution_convert_fusion.6
  109.5 29.6 %shard_map.188 = (f32[128,768]{1,0:T(8,128)}, bf16[4,128,768]{2,1,0:T(8,128)(2,1)}, bf16[8,96,1536]{2,1,0:T(8,128)(2,1)}) custom-call(bf16[4,128,768]{2,1,0:T(8,128)(2,1)} %bitcast.89, bf16[128,768]{1,0:T(8,128)(2,1)} %frames.5, f32[1,768]{1,0:T(1,128)} %get-tuple-element.121.gain, f32[1,768]{1,0:T(1,128)} %get-tuple-element.110.shift, ...), custom_call_target="tpu_custom_call" | custom-call | tf_op jit(solution)/shard_map/pallas_call | solution.py:473
  139.1 2.5 multiply_convert_fusion
  141.6 1.7 convolution_convert_fusion.4
  144.5 1.7 convolution_convert_fusion.3
  146.5 2.0 convolution_convert_fusion
  148.8 1.9 convolution_convert_fusion.1
  150.7 1.6 pad_maximum_fusion.grads
  152.3 31.8 %shard_map.189 = (bf16[128,768]{1,0:T(8,128)(2,1)}, f32[128,768]{1,0:T(8,128)}, bf16[4,128,768]{2,1,0:T(8,128)(2,1)}, f32[4,768]{1,0:T(4,128)}, bf16[4,96,1536]{2,1,0:T(8,128)(2,1)}) custom-call(bf16[4,128,768]{2,1,0:T(8,128)(2,1)} %bitcast.95, bf16[4,128,768]{2,1,0:T(8,128)(2,1)} %bitcast.96, f32[128,768]{1,0:T(8,128)} %get-tuple-element.43.hidden, ...), custom_call_target="tpu_custom_call" | custom-call | tf_op jit(solution)/shard_map/pallas_call | solution.py:473
  184.1 1.6 convolution_convert_fusion.8
  186.6 1.7 sub.24
  188.3 1.8 fusion.5.kid
  191.4 55.6 %shard_map.190 = (bf16[512,192]{1,0:T(8,128)(2,1)}, f32[512,384]{1,0:T(8,128)}, f32[96,1536]{1,0:T(8,128)}, f32[96,192]{1,0:T(8,128)}) custom-call(bf16[512,192]{1,0:T(8,128)(2,1)} %slice.120.queries, bf16[7,512,384]{2,1,0:T(8,128)(2,1)} %get-tuple-element.45.window, bf16[512,192]{1,0:T(8,128)(2,1)} %copy.68.grad_out, f32[3,512]{1,0:T(4,128)} %get-tuple-element.47.lse, ...), custom_call_target="tpu_custom_call" | custom-call | tf_op jit(solution)/shard_map/pallas_call | solution.py:473
  247.0 1.2 convert_element_type.57
  248.2 2.8 convolution_convert_fusion.5
  251.9 1.3 copy.69
  254.2 1.3 concatenate.25.vec_in
  255.5 47.2 %shard_map.191 = (bf16[128,768]{1,0:T(8,128)(2,1)}, f32[96,576]{1,0:T(8,128)}, f32[16,768]{1,0:T(8,128)}) custom-call(bf16[4,128,768]{2,1,0:T(8,128)(2,1)} %bitcast.94, bf16[128,768]{1,0:T(8,128)(2,1)} %frames.5, f32[128,768]{1,0:T(8,128)} %get-tuple-element.51.dh, f32[1,768]{1,0:T(1,128)} %get-tuple-element.120.gain, bf16[8,96,576]{2,1,0:T(8,128)(2,1)} %bitcast.86, ...), custom_call_target="tpu_custom_call" | custom-call | tf_op jit(solution)/shard_map/pallas_call | solution.py:473
  (89 shorter events, 19.2 us)
Async XLA Ops:
  0.6 0.7 copy-start
  30.4 4.0 %copy-start.16 = (s32[6]{0:T(128)S(1)}, s32[6]{0:T(128)}, u32[]{:S(2)}) copy-start(s32[6]{0:T(128)} %param.12) | copy-start | bytes 76
  32.6 5.2 %copy-start.13 = (bf16[1,192,96]{2,1,0:T(8,128)(2,1)S(1)}, bf16[1,192,96]{2,1,0:T(8,128)(2,1)}, u32[]{:S(2)}) copy-start(bf16[1,192,96]{2,1,0:T(8,128)(2,1)} %param.14) | copy-start | bytes 110596
  32.6 6.0 %copy-start.10 = (bf16[1,768,96]{1,2,0:T(8,128)(2,1)S(1)}, bf16[1,768,96]{1,2,0:T(8,128)(2,1)}, u32[]{:S(2)}) copy-start(bf16[1,768,96]{1,2,0:T(8,128)(2,1)} %param.16) | copy-start | bytes 442372
  32.6 6.0 %copy-start.11 = (bf16[1,96,768]{2,1,0:T(8,128)(2,1)S(1)}, bf16[1,96,768]{2,1,0:T(8,128)(2,1)}, u32[]{:S(2)}) copy-start(bf16[1,96,768]{2,1,0:T(8,128)(2,1)} %param.15) | copy-start | bytes 442372
  139.1 2.6 copy-start.17
  141.6 1.7 copy-start.21
  141.6 1.7 copy-start.4
  144.4 1.7 copy-start.20
  146.5 2.0 copy-start.5
  152.3 31.8 %copy-start.2 = (bf16[8,96,192]{2,1,0:T(8,128)(2,1)S(1)}, bf16[8,96,192]{2,1,0:T(8,128)(2,1)}, u32[]{:S(2)}) copy-start(bf16[8,96,192]{2,1,0:T(8,128)(2,1)} %get-tuple-element.37) | copy-start | bytes 884740
  188.2 1.8 copy-start.1
  188.2 1.8 copy-start.3
  191.4 56.8 %copy-start.18 = (bf16[8,96,576]{2,1,0:T(8,128)(2,1)S(1)}, bf16[8,96,576]{2,1,0:T(8,128)(2,1)}, u32[]{:S(2)}) copy-start(bf16[8,96,576]{2,1,0:T(8,128)(2,1)} %get-tuple-element.35) | copy-start | bytes 2654212
  248.1 2.8 copy-start.7
  248.1 2.8 copy-start.19
  251.9 1.3 copy-start.15
  255.5 49.2 %copy-start.12 = (f32[96,192]{1,0:T(8,128)S(1)}, f32[96,192]{1,0:T(8,128)}, u32[]{:S(2)}) copy-start(f32[96,192]{1,0:T(8,128)} %get-tuple-element.55) | copy-start | bytes 221188
  255.5 50.0 %copy-start.6 = (f32[96,1536]{1,0:T(8,128)S(1)}, f32[96,1536]{1,0:T(8,128)}, u32[]{:S(2)}) copy-start(f32[96,1536]{1,0:T(8,128)} %get-tuple-element.56) | copy-start | bytes 1769476
  302.7 3.7 %copy-start.14 = (f32[16,768]{1,0:T(8,128)S(1)}, f32[16,768]{1,0:T(8,128)}, u32[]{:S(2)}) copy-start(f32[16,768]{1,0:T(8,128)} %get-tuple-element.57) | copy-start | bytes 147460
  302.7 5.5 %copy-start.8 = (bf16[128,768]{1,0:T(8,128)(2,1)S(1)}, bf16[128,768]{1,0:T(8,128)(2,1)}, u32[]{:S(2)}) copy-start(bf16[128,768]{1,0:T(8,128)(2,1)} %get-tuple-element.134) | copy-start | bytes 589828
  302.7 6.1 %copy-start.9 = (bf16[128,768]{1,0:T(8,128)(2,1)S(1)}, bf16[128,768]{1,0:T(8,128)(2,1)}, u32[]{:S(2)}) copy-start(bf16[128,768]{1,0:T(8,128)(2,1)} %get-tuple-element.135) | copy-start | bytes 589828
